TPU v7x, 32 devices: a whole 2x2x4 slice. The times are simulated.
32 devices in a mesh: dp: 8 (over y, x, core), mp: 4 (over z).
Axes of the slice: x: 2, y: 2, z: 4, core: 2. Of those that a mesh axis runs over, the one named last changes fastest.
Arguments:
- tokens: bfloat16 [8192, 2048], P(('dp', 'mp')), may hold values from -6 to 6
- norm_gain: float32 [2048], replicated, may hold values from 0.1 to 1.9
- mlp_gain: float32 [2048], replicated, may hold values from 0.1 to 1.9
- lengths: int32 [8], P('dp'), may hold values from 1 to 1024, as said below
- log_decay: float32 [8192, 8], P('dp'), as said below
- query_master: float32 [2048, 2048], P(('dp', 'mp')), may hold values from -0.125 to 0.125
- key_master: float32 [2048, 2048], P(('dp', 'mp')), may hold values from -0.125 to 0.125
- value_master: float32 [2048, 4096], P(('dp', 'mp')), may hold values from -0.125 to 0.125
- swish_master: float32 [2048, 4096], P(('dp', 'mp')), may hold values from -0.125 to 0.125
- output_master: float32 [4096, 2048], P(None, ('dp', 'mp')), may hold values from -0.09375 to 0.09375
- ffn_gate_master: float32 [2048, 4096], P(('dp', 'mp')), may hold values from -0.125 to 0.125
- ffn_up_master: float32 [2048, 4096], P(('dp', 'mp')), may hold values from -0.125 to 0.125
Outputs:
- residual: bfloat16 [8192, 2048], P(('dp', 'mp'))
- hidden: bfloat16 [8192, 4096], P('dp', 'mp')
Inputs may be any that keep to these rules, and one draw needn't show every extreme that they name: `lengths`: given length of each prompt; in every draw some prompt has exactly 1024 tokens and some has 1. `log_decay`: Negative.
All inputs are finite; a program needn't handle non-finite values.
Results may differ from a plain program's by a relative error of at most 0.023.
Values may be sent and summed in bfloat16 or wider, within the bound.
No kernel may reach another device: no remote copies, remote signals or barrier semaphores. Data moves between devices by JAX's collectives and lax.ppermute only.
A program may use at most 128 MiB of HBM per device.

v0:
```python
import math

import jax
import jax.numpy as jnp
from jax import lax
from jax.sharding import PartitionSpec as P

H = 8
DK = 256
DV = 512
REQUEST_SPAN = 1024
BLOCK = 512
PROMPTS_DP = 1


def rms_rows(row_block, gain_vec):
    values = row_block.astype(jnp.float32)
    scale = lax.rsqrt(jnp.mean(values * values, axis=-1, keepdims=True) + 1e-06)
    return (values * scale * gain_vec).astype(jnp.bfloat16)


def rotate(values, places):
    columns = values.shape[1]
    channel = jnp.arange(columns, dtype=jnp.int32) % DK
    paired = (channel // 2 * 2).astype(jnp.float32)
    frequency = jnp.exp(paired * (-math.log(10000.0) / DK))
    angles = places.astype(jnp.float32)[:, None] * frequency[None, :]
    couples = values.reshape(values.shape[0], columns // 2, 2)
    turned = jnp.stack([-couples[:, :, 1], couples[:, :, 0]], axis=-1).reshape(values.shape)
    return values * jnp.cos(angles) + turned * jnp.sin(angles)


def spread_heads(matrix, width, copies):
    if copies == 1:
        return matrix
    row_total = matrix.shape[0]
    per_head = jnp.repeat(matrix.reshape(row_total, H, width), copies, axis=1)
    return per_head.reshape(row_total, H * copies * width)


def trainer_order(block_rows, dp_count, mp_count):
    row_total, columns = block_rows.shape
    split_rows = block_rows.reshape(mp_count, dp_count, row_total // (dp_count * mp_count), columns)
    return split_rows.transpose(1, 0, 2, 3).reshape(row_total, columns)


def retain_block(offset, q_block, k_block, v_block, run_query, run_key):
    scores = jnp.einsum(
        "thd,shd->hts", q_block, k_block, preferred_element_type=jnp.float32
    ) * DK ** (-0.5)
    decay_gap = run_query.T[:, :, None] - run_key.T[:, None, :]
    causal_mask = (offset + jnp.arange(q_block.shape[0], dtype=jnp.int32))[:, None] >= jnp.arange(
        k_block.shape[0], dtype=jnp.int32
    )[None, :]
    weights = (scores * jnp.exp(jnp.where(causal_mask[None], decay_gap, -jnp.inf))).astype(
        jnp.bfloat16
    )
    return jnp.einsum("hts,shd->thd", weights, v_block, preferred_element_type=jnp.float32)


def per_device(
    tokens,
    norm_gain,
    mlp_gain,
    lengths,
    log_decay,
    query_master,
    key_master,
    value_master,
    swish_master,
    output_master,
    ffn_gate_master,
    ffn_up_master,
):
    mp_count = lax.axis_size("mp")
    dp_count = lax.axis_size("dp")
    mp_index = lax.axis_index("mp")
    head_share = max(1, mp_count // H)
    local_heads = max(1, H // mp_count)
    partner_bit = mp_index % head_share
    group_rows = PROMPTS_DP * REQUEST_SPAN
    value_width = DV // head_share
    m_query = spread_heads(query_master.astype(jnp.bfloat16), DK, head_share)
    m_key = spread_heads(key_master.astype(jnp.bfloat16), DK, head_share)
    m_value = spread_heads(value_master.astype(jnp.bfloat16), DV, head_share)
    m_swish = swish_master.astype(jnp.bfloat16)
    m_output = output_master.T.astype(jnp.bfloat16)
    m_ffn_gate = ffn_gate_master.astype(jnp.bfloat16)
    m_ffn_up = ffn_up_master.astype(jnp.bfloat16)
    r_query, r_key, r_value, r_swish, r_output, r_gate, r_up = (
        lax.all_gather(m_query, "dp", axis=0, tiled=True),
        lax.all_gather(m_key, "dp", axis=0, tiled=True),
        lax.all_gather(m_value, "dp", axis=0, tiled=True),
        lax.all_gather(m_swish, "dp", axis=0, tiled=True),
        lax.all_gather(m_output, "dp", axis=0, tiled=True),
        lax.all_gather(m_ffn_gate, "dp", axis=0, tiled=True),
        lax.all_gather(m_ffn_up, "dp", axis=0, tiled=True),
    )
    owned_parts = (
        lax.all_to_all(r_query, "mp", split_axis=1, concat_axis=0, tiled=True),
        lax.all_to_all(r_key, "mp", split_axis=1, concat_axis=0, tiled=True),
        lax.all_to_all(r_value, "mp", split_axis=1, concat_axis=0, tiled=True),
        lax.all_to_all(r_swish, "mp", split_axis=1, concat_axis=0, tiled=True),
        lax.all_to_all(r_output, "mp", split_axis=1, concat_axis=0, tiled=True),
        lax.all_to_all(r_gate, "mp", split_axis=1, concat_axis=0, tiled=True),
        lax.all_to_all(r_up, "mp", split_axis=1, concat_axis=0, tiled=True),
    )
    server = [trainer_order(owned, dp_count, mp_count) for owned in owned_parts]
    w_query, w_key, w_value, w_swish, w_output, w_ffn_gate, w_ffn_up = server
    width_qk = w_query.shape[1]
    width_value = w_value.shape[1]
    merged_weights = jnp.concatenate([w_query, w_key, w_value, w_swish], axis=1)
    normed_in = rms_rows(tokens, norm_gain)
    shard_piece = lax.all_gather(normed_in, "mp", axis=0, tiled=True)
    places = jnp.arange(shard_piece.shape[0], dtype=jnp.int32) % REQUEST_SPAN
    projected_rows = jnp.dot(shard_piece, merged_weights, preferred_element_type=jnp.float32)
    rotated_query = rotate(projected_rows[:, :width_qk], places)
    rotated_key = rotate(projected_rows[:, width_qk : 2 * width_qk], places)
    projected = jnp.concatenate(
        [rotated_query, rotated_key, projected_rows[:, 2 * width_qk :]], axis=1
    ).astype(jnp.bfloat16)
    queries = projected[:, :width_qk]
    key_rows = projected[:, width_qk : 2 * width_qk]
    value_rows = projected[:, 2 * width_qk : 2 * width_qk + width_value]
    gate_rows = projected[:, 2 * width_qk + width_value :]
    head_first = mp_index // head_share * local_heads
    decay_cols = lax.dynamic_slice_in_dim(log_decay, head_first, local_heads, 1)
    running = jnp.cumsum(decay_cols.reshape(PROMPTS_DP, REQUEST_SPAN, local_heads), axis=1)
    query_four = queries.reshape(PROMPTS_DP, REQUEST_SPAN, local_heads, DK)
    key_four = key_rows.reshape(PROMPTS_DP, REQUEST_SPAN, local_heads, DK)
    value_four = value_rows.reshape(PROMPTS_DP, REQUEST_SPAN, local_heads, DV)

    def one_prompt(prompt_items):
        q_prompt, k_prompt, v_prompt, run_prompt, length_prompt = prompt_items
        outputs = []
        for block_index in range(REQUEST_SPAN // BLOCK):
            low_row = block_index * BLOCK
            top_row = low_row + BLOCK
            operands = (
                q_prompt[low_row:top_row],
                k_prompt[:top_row],
                v_prompt[:top_row],
                run_prompt[low_row:top_row],
                run_prompt[:top_row],
            )
            block_out = retain_block(low_row, *operands)
            outputs.append(block_out)
        return jnp.concatenate(outputs, axis=0)

    retained = lax.map(one_prompt, (query_four, key_four, value_four, running, lengths))
    retained = retained.reshape(group_rows, local_heads, DV)
    channel_mean = jnp.mean(retained, axis=-1, keepdims=True)
    spread = jnp.mean(retained * retained, axis=-1, keepdims=True) - channel_mean * channel_mean
    normed_heads = (retained - channel_mean) * lax.rsqrt(spread + 1e-05)
    if head_share > 1:
        normed_heads = lax.dynamic_slice_in_dim(
            normed_heads, partner_bit * value_width, value_width, 2
        )
    live_rows = jnp.arange(group_rows, dtype=jnp.int32) % REQUEST_SPAN < jnp.repeat(
        lengths, REQUEST_SPAN
    )
    gated = jnp.where(
        live_rows[:, None],
        jax.nn.silu(gate_rows.astype(jnp.float32))
        * normed_heads.reshape(group_rows, local_heads * value_width),
        0.0,
    ).astype(jnp.bfloat16)
    branch = lax.psum_scatter(
        lax.dot_general(
            gated, w_output, (((1,), (1,)), ((), ())), preferred_element_type=jnp.float32
        ).astype(jnp.bfloat16),
        "mp",
        scatter_dimension=0,
        tiled=True,
    ).astype(jnp.float32)
    residual = (tokens.astype(jnp.float32) + branch).astype(jnp.bfloat16)
    normed_mid = rms_rows(residual, mlp_gain)
    w_gate_up = jnp.concatenate([w_ffn_gate, w_ffn_up], axis=1)
    split_at = w_ffn_gate.shape[1]
    gate_up = jnp.dot(
        lax.all_gather(normed_mid, "mp", axis=0, tiled=True),
        w_gate_up,
        preferred_element_type=jnp.float32,
    )
    hidden = (jax.nn.silu(gate_up[:, :split_at]) * gate_up[:, split_at:]).astype(jnp.bfloat16)
    return (residual, hidden)


def solution(mesh):
    placed = (
        P(("dp", "mp"), None),
        P(),
        P(),
        P("dp"),
        P("dp", None),
        P(("dp", "mp"), None),
        P(("dp", "mp"), None),
        P(("dp", "mp"), None),
        P(("dp", "mp"), None),
        P(None, ("dp", "mp")),
        P(("dp", "mp"), None),
        P(("dp", "mp"), None),
    )
    return jax.shard_map(
        per_device,
        mesh=mesh,
        in_specs=placed,
        out_specs=(P(("dp", "mp"), None), P("dp", "mp")),
        check_vma=False,
    )
```

profile of v0, /device:TPU:0, one launch (start us, length us, event | category | flops | bytes accessed | tf_op | source)
XLA Modules:
  0.0 929.8 jit_solution(10784598540507466584)
XLA Ops:
  15.1 26.0 %all-gather.14.cloned.1.call-done = bf16[512,2048]{1,0:T(8,128)(2,1)} async-done(((bf16[64,2048]{1,0:T(8,128)(2,1)}), bf16[512,2048]{1,0:T(8,128)(2,1)}) %all-gather.14.cloned.1.call-update) | async-done | bytes 2097168 | tf_op jit(solution)/shard_map/all_gather | solution.py:92
  41.1 3.9 copy.81
  45.0 4.6 all-to-all-start.1
  50.0 21.0 %all-gather.12.cloned.1.call-done = bf16[512,2048]{1,0:T(8,128)(2,1)} async-done(((bf16[64,2048]{1,0:T(8,128)(2,1)}), bf16[512,2048]{1,0:T(8,128)(2,1)}) %all-gather.12.cloned.1.call-update) | async-done | bytes 2097168 | tf_op jit(solution)/shard_map/all_gather | solution.py:91
  70.9 3.9 copy.78
  74.9 23.4 %all-to-all-done.1 = bf16[512,4,512]{0,2,1:T(8,128)(2,1)S(1)} async-done(((bf16[512,4,512]{0,2,1:T(8,128)(2,1)}), bf16[512,4,512]{0,2,1:T(8,128)(2,1)S(1)}, u32[]{:S(2)}, u32[]{:S(2)}) %all-to-all-start.1) | async-done | bytes 2097184 | tf_op jit(solution)/shard_map/all_to_all | solution.py:101
  98.3 4.5 all-to-all-start
  104.1 5.5 all-gather.16.cloned.1.call-done
  109.6 6.5 copy.84
  116.1 34.5 %all-to-all-done = bf16[512,4,512]{0,2,1:T(8,128)(2,1)} async-done(((bf16[512,4,512]{0,2,1:T(8,128)(2,1)}), bf16[512,4,512]{0,2,1:T(8,128)(2,1)}, u32[]{:S(2)}, u32[]{:S(2)}) %all-to-all-start) | async-done | bytes 2097184 | tf_op jit(solution)/shard_map/all_to_all | solution.py:100
  150.6 4.9 all-to-all-start.2
  157.7 6.6 copy.87
  164.3 143.0 %all-to-all-done.2 = bf16[512,4,1024]{0,2,1:T(8,128)(2,1)} async-done(((bf16[512,4,1024]{0,2,1:T(8,128)(2,1)}), bf16[512,4,1024]{0,2,1:T(8,128)(2,1)}, u32[]{:S(2)}, u32[]{:S(2)}) %all-to-all-start.2) | async-done | bytes 4194336 | tf_op jit(solution)/shard_map/all_to_all | solution.py:102
  307.3 4.9 all-to-all-start.3
  317.4 2.4 copy.82
  319.8 3.1 copy.83
  322.9 2.8 copy.79
  327.2 6.5 copy.104
  333.7 6.3 copy.85
  340.0 4.9 copy.86
  344.9 60.7 %all-to-all-done.3 = bf16[512,4,1024]{0,2,1:T(8,128)(2,1)} async-done(((bf16[512,4,1024]{0,2,1:T(8,128)(2,1)}), bf16[512,4,1024]{0,2,1:T(8,128)(2,1)}, u32[]{:S(2)}, u32[]{:S(2)}) %all-to-all-start.3) | async-done | bytes 4194336 | tf_op jit(solution)/shard_map/all_to_all | solution.py:103
  405.5 4.9 all-to-all-start.4
  410.7 6.3 copy.88
  417.0 5.2 copy.89
  422.2 21.0 %fusion.88 = (bf16[1024,3072]{1,0:T(8,128)(2,1)}, f32[1024,3072]{1,0:T(8,128)}) fusion(bf16[1024,2048]{1,0:T(8,128)(2,1)} %all-gather.10.cloned.1.call-done, bf16[2048,1024]{1,0:T(8,128)(2,1)} %bitcast.146, bf16[2048,1024]{1,0:T(8,128)(2,1)} %bitcast.142, bf16[2048,512]{1,0:T(8,128)(2,1)S(1)} %bitcast.150, bf16[2048,512]{1,0:T(8,128)(2,1)} %bitcast.151), kind=kOutput, calls=%fused_computation.123 | convolution fusion | flops 12938379264 | bytes 35651584 | tf_op jit(solution)/shard_map/dot_general | solution.py:116
  445.0 2.3 slice.124
  447.3 4.7 fusion.86
  452.0 2.9 copy.92
  454.9 3.9 reshape.274
  458.7 4.3 slice_negate_fusion
  463.0 3.2 pad_maximum_fusion.2
  466.3 3.7 reshape.275
  470.0 2.9 copy.93
  472.9 2.9 copy.90
  475.8 3.4 reshape.272
  479.2 4.3 slice_negate_fusion.1
  483.5 3.2 pad_maximum_fusion.1
  486.7 3.7 reshape.273
  490.4 2.9 copy.91
  493.3 2.7 copy.115
  496.1 10.3 %fusion.29 = (bf16[1024,512]{1,0:T(8,128)(2,1)S(1)}, bf16[1024,512]{1,0:T(8,128)(2,1)S(1)}) fusion(f32[1024,512]{1,0:T(8,128)} %copy.91, f32[512]{0:T(512)S(1)} %fusion.70, f32[1024]{0:T(1024)S(1)} %fusion.63, f32[1024,3072]{1,0:T(8,128)} %get-tuple-element.41, f32[1024,512]{1,0:T(8,128)} %copy.93), kind=kLoop, calls=%fused_computation.44 | loop fusion | flops 4718592 | bytes 10491904 | tf_op jit(solution)/shard_map/convert
  510.5 2.8 fusion.38
  513.3 5.8 fusion.39
  522.4 2.9 sub.82
  525.2 3.0 copy.122
  529.3 2.9 mul.192
  532.2 3.0 copy.123
  535.2 2.9 copy.116
  539.9 6.3 copy.105
  546.2 5.2 copy.106
  552.5 11.1 %convolution_convert_fusion = bf16[1024,2048]{1,0:T(8,128)(2,1)} fusion(bf16[2048,1024]{1,0:T(8,128)(2,1)} %bitcast.147, f32[1024,1024]{1,0:T(8,128)} %bitcast.144, f32[1024,1024]{1,0:T(8,128)S(1)} %bitcast.143, f32[512,1024]{1,0:T(8,128)S(1)} %copy-done.8, f32[512,1024]{1,0:T(8,128)S(1)} %copy-done.9, bf16[1024,3072]{1,0:T(8,128)(2,1)} %get-tuple-element.40, ...), kind=kOutput, calls=%fused_computation.27 | convolution fusion | flops 4308598784 | bytes 23069696 | tf_op jit(solution)/shard_map/dot_general | solution.py:169
  563.6 6.5 copy.107
  570.0 5.0 all-to-all-start.5
  575.1 6.5 copy.110
  581.5 119.1 %reduce-scatter.2.cloned.1.call-done = bf16[256,2048]{1,0:T(8,128)(2,1)} async-done(((bf16[1024,2048]{1,0:T(8,128)(2,1)}), bf16[256,2048]{1,0:T(8,128)(2,1)}) %reduce-scatter.2.cloned.1.call-update) | async-done | bytes 1048592 | tf_op jit(solution)/shard_map/reduce_scatter | solution.py:168
  702.4 28.0 %all-to-all-done.5 = bf16[512,4,1024]{0,2,1:T(8,128)(2,1)} async-done(((bf16[512,4,1024]{0,2,1:T(8,128)(2,1)}), bf16[512,4,1024]{0,2,1:T(8,128)(2,1)}, u32[]{:S(2)}, u32[]{:S(2)}) %all-to-all-start.5) | async-done | bytes 4194336 | tf_op jit(solution)/shard_map/all_to_all | solution.py:105
  730.4 5.0 all-to-all-start.6
  736.8 6.3 copy.108
  743.1 4.9 copy.109
  748.0 148.2 %all-to-all-done.6 = bf16[512,4,1024]{0,2,1:T(8,128)(2,1)} async-done(((bf16[512,4,1024]{0,2,1:T(8,128)(2,1)}), bf16[512,4,1024]{0,2,1:T(8,128)(2,1)}, u32[]{:S(2)}, u32[]{:S(2)}) %all-to-all-start.6) | async-done | bytes 4194336 | tf_op jit(solution)/shard_map/all_to_all | solution.py:106
  896.2 6.3 copy.111
  902.5 4.9 copy.112
  907.4 12.6 %fusion.8 = f32[1024,2048]{1,0:T(8,128)S(1)} fusion(bf16[1024,2048]{1,0:T(8,128)(2,1)} %all-gather.22.cloned.1.call-done, bf16[2048,1024]{1,0:T(8,128)(2,1)} %bitcast.148, bf16[2048,1024]{1,0:T(8,128)(2,1)} %bitcast.145), kind=kOutput, calls=%fused_computation.8 | convolution fusion | flops 8606711808 | bytes 20971520 | tf_op jit(solution)/shard_map/dot_general | solution.py:180
  920.0 2.7 fusion.17
  (95 shorter events, 34.2 us)
Async XLA Ops:
  7.2 307.2 %copy-start = (f32[1024,8]{0,1:T(8,128)S(1)}, f32[1024,8]{0,1:T(8,128)}, u32[]{:S(2)}) copy-start(f32[1024,8]{0,1:T(8,128)} %param.16) | copy-start | bytes 98308
  7.2 6.1 copy-start.10
  7.2 7.0 copy-start.11
  7.2 33.9 %all-gather.14.cloned.1.call-start = ((), (), s32[]{:S(2)}) async-start(), calls=%async_computation.10 | async-start | bytes 2359296 | tf_op jit(solution)/shard_map/all_gather | solution.py:92
  9.2 61.8 %all-gather.12.cloned.1.call-start = ((), (), s32[]{:S(2)}) async-start(), calls=%async_computation.9 | async-start | bytes 2359296 | tf_op jit(solution)/shard_map/all_gather | solution.py:91
  11.0 98.6 %all-gather.16.cloned.1.call-start = ((), (), s32[]{:S(2)}) async-start(), calls=%async_computation.11 | async-start | bytes 4718592 | tf_op jit(solution)/shard_map/all_gather | solution.py:93
  13.2 144.5 %all-gather.18.cloned.1.call-start = ((), (), s32[]{:S(2)}) async-start(), calls=%async_computation.12 | async-start | bytes 4718592 | tf_op jit(solution)/shard_map/all_gather | solution.py:94
  14.2 313.0 %all-gather.20.cloned.1.call-start = ((), (), s32[]{:S(2)}) async-start(), calls=%async_computation.13 | async-start | bytes 4718592 | tf_op jit(solution)/shard_map/all_gather | solution.py:95
  15.1 34.6 %copy-start.2 = (bf16[256,2048]{1,0:T(8,128)(2,1)S(1)}, bf16[256,2048]{1,0:T(8,128)(2,1)}, u32[]{:S(2)}) copy-start(bf16[256,2048]{1,0:T(8,128)(2,1)} %param.12) | copy-start | bytes 3145732
  45.0 53.2 %all-to-all-start.1 = ((bf16[512,4,512]{0,2,1:T(8,128)(2,1)}), bf16[512,4,512]{0,2,1:T(8,128)(2,1)S(1)}, u32[]{:S(2)}, u32[]{:S(2)}) async-start(bf16[512,4,512]{0,2,1:T(8,128)(2,1)} %bitcast.139), calls=%async_computation.1 | async-start | bytes 4194304 | tf_op jit(solution)/shard_map/all_to_all | solution.py:101
  49.9 52.9 %copy-start.12 = (f32[2048]{0:T(1024)S(1)}, f32[2048]{0:T(1024)}, u32[]{:S(2)}) copy-start(f32[2048]{0:T(1024)} %param.13) | copy-start | bytes 24580
  98.3 52.3 %all-to-all-start = ((bf16[512,4,512]{0,2,1:T(8,128)(2,1)}), bf16[512,4,512]{0,2,1:T(8,128)(2,1)}, u32[]{:S(2)}, u32[]{:S(2)}) async-start(bf16[512,4,512]{0,2,1:T(8,128)(2,1)} %bitcast.136), calls=%async_computation | async-start | bytes 4194304 | tf_op jit(solution)/shard_map/all_to_all | solution.py:100
  102.7 319.4 %all-gather.10.cloned.1.call-start = ((), (), s32[]{:S(2)}) async-start(), calls=%async_computation.8 | async-start | bytes 5242880 | tf_op jit(solution)/shard_map/all_gather | solution.py:114
  150.6 156.7 %all-to-all-start.2 = ((bf16[512,4,1024]{0,2,1:T(8,128)(2,1)}), bf16[512,4,1024]{0,2,1:T(8,128)(2,1)}, u32[]{:S(2)}, u32[]{:S(2)}) async-start(bf16[512,4,1024]{0,2,1:T(8,128)(2,1)} %bitcast.124), calls=%async_computation.2 | async-start | bytes 8388608 | tf_op jit(solution)/shard_map/all_to_all | solution.py:102
  155.5 408.1 %all-gather.24.cloned.1.call-start = ((), (), s32[]{:S(2)}) async-start(), calls=%async_computation.16 | async-start | bytes 4718592 | tf_op jit(solution)/shard_map/all_gather | solution.py:96
  307.3 98.2 %all-to-all-start.3 = ((bf16[512,4,1024]{0,2,1:T(8,128)(2,1)}), bf16[512,4,1024]{0,2,1:T(8,128)(2,1)}, u32[]{:S(2)}, u32[]{:S(2)}) async-start(bf16[512,4,1024]{0,2,1:T(8,128)(2,1)} %bitcast.122), calls=%async_computation.3 | async-start | bytes 8388608 | tf_op jit(solution)/shard_map/all_to_all | solution.py:103
  312.2 262.8 %all-gather.26.cloned.1.call-start = ((), (), s32[]{:S(2)}) async-start(), calls=%async_computation.17 | async-start | bytes 4718592 | tf_op jit(solution)/shard_map/all_gather | solution.py:97
  405.5 134.3 %all-to-all-start.4 = ((bf16[512,4,1024]{0,2,1:T(8,128)(2,1)}), bf16[512,4,1024]{0,2,1:T(8,128)(2,1)}, u32[]{:S(2)}, u32[]{:S(2)}) async-start(bf16[512,4,1024]{0,2,1:T(8,128)(2,1)} %bitcast.121), calls=%async_computation.4 | async-start | bytes 8388608 | tf_op jit(solution)/shard_map/all_to_all | solution.py:104
  410.4 290.2 %reduce-scatter.2.cloned.1.call-start = ((), (), s32[]{:S(2)}) async-start(), calls=%async_computation.14 | async-start | bytes 5242880 | tf_op jit(solution)/shard_map/reduce_scatter | solution.py:168
  417.0 5.2 copy-start.7
  496.0 12.1 %copy-start.4 = (bf16[512,1024]{1,0:T(8,128)(2,1)S(1)}, bf16[512,1024]{1,0:T(8,128)(2,1)}, u32[]{:S(2)}) copy-start(bf16[512,1024]{1,0:T(8,128)(2,1)} %slice.124) | copy-start | bytes 3145732
  506.3 1.0 copy-start.6
  546.2 5.2 copy-start.3
  546.2 5.2 copy-start.8
  546.2 6.2 copy-start.9
  570.0 160.4 %all-to-all-start.5 = ((bf16[512,4,1024]{0,2,1:T(8,128)(2,1)}), bf16[512,4,1024]{0,2,1:T(8,128)(2,1)}, u32[]{:S(2)}, u32[]{:S(2)}) async-start(bf16[512,4,1024]{0,2,1:T(8,128)(2,1)} %bitcast.125), calls=%async_computation.6 | async-start | bytes 8388608 | tf_op jit(solution)/shard_map/all_to_all | solution.py:105
  702.4 33.1 %copy-start.5 = (bf16[256,2048]{1,0:T(8,128)(2,1)}, bf16[256,2048]{1,0:T(8,128)(2,1)S(1)}, u32[]{:S(2)}) copy-start(bf16[256,2048]{1,0:T(8,128)(2,1)S(1)} %get-tuple-element.17) | copy-start | bytes 3145732
  730.4 5.1 copy-start.13
  730.4 165.8 %all-to-all-start.6 = ((bf16[512,4,1024]{0,2,1:T(8,128)(2,1)}), bf16[512,4,1024]{0,2,1:T(8,128)(2,1)}, u32[]{:S(2)}, u32[]{:S(2)}) async-start(bf16[512,4,1024]{0,2,1:T(8,128)(2,1)} %bitcast.123), calls=%async_computation.7 | async-start | bytes 8388608 | tf_op jit(solution)/shard_map/all_to_all | solution.py:106
  735.4 172.0 %all-gather.22.cloned.1.call-start = ((), (), s32[]{:S(2)}) async-start(), calls=%async_computation.15 | async-start | bytes 5242880 | tf_op jit(solution)/shard_map/all_gather | solution.py:181
  907.4 15.3 %copy-start.1 = (f32[1024,8]{0,1:T(8,128)S(1)}, f32[1024,8]{0,1:T(8,128)}, u32[]{:S(2)}) copy-start(f32[1024,8]{0,1:T(8,128)} %param.16) | copy-start | bytes 98308
Sparse Core Ops, SparseCore 0:
  10.5 30.5 all-gather.13
  43.0 27.8 all-gather.11
  72.8 36.7 all-gather.15
  111.3 36.7 all-gather.17
  149.8 36.7 all-gather.19
  188.6 154.7 all-gather.9
  345.3 35.0 all-gather.23
  382.3 36.7 all-gather.25
  563.7 136.8 reduce-scatter.1
  738.2 148.0 all-gather.21
where the time goes:
time: 938 us; the launch traced here: 930 us
  waiting for transfers between devices  610 us (65%)
  local copies, waits for them, and re-layouts  169 us (18%)
  matrix products  53.2 us (6%)
  other arithmetic  48.7 us (5%)
  starting transfers between devices  34.3 us (4%)
  between operations  15.4 us (2%)
    all_to_all x1, waiting for transfers between devices, per_device(): lax.all_to_all(r_up, 'mp', split_axis=1, concat_axis=0, tiled=True)  148 us
    all_to_all x1, waiting for transfers between devices, per_device(): lax.all_to_all(r_value, 'mp', split_axis=1, concat_axis=0, tiled=True)  143 us
    reduce_scatter x1, waiting for transfers between devices, per_device(): lax.psum_scatter(lax.dot_general(gated, w_output, (((1,), (1,)), ((), ())...  119 us
    all_to_all x1, waiting for transfers between devices, per_device(): lax.all_to_all(r_swish, 'mp', split_axis=1, concat_axis=0, tiled=True)  60.7 us
    all_to_all x1, waiting for transfers between devices, per_device(): lax.all_to_all(r_query, 'mp', split_axis=1, concat_axis=0, tiled=True)  34.5 us
    transpose x7, local copies, waits for them, and re-layouts, trainer_order(): return split_rows.transpose(1, 0, 2, 3).reshape(row_total, columns)  29.7 us
    all_to_all x1, waiting for transfers between devices, per_device(): lax.all_to_all(r_gate, 'mp', split_axis=1, concat_axis=0, tiled=True)  28 us
    all_gather x1, waiting for transfers between devices, per_device(): lax.all_gather(m_key, 'dp', axis=0, tiled=True)  26 us
  transfers between devices with their start and end apart: 17, of which 10 were waited for; matrix products, arithmetic and copies ran while one was open for 27% of the time, Pallas kernels for 0%

commit v1 on v0

v1 whole, which is shorter than its diff:
```python
import math

import jax
import jax.numpy as jnp
from jax import lax
from jax.experimental import pallas as pl
from jax.experimental.pallas import tpu as pltpu
from jax.sharding import PartitionSpec as P

H = 8
DK = 256
DV = 512
SPAN = 1024
HALF = DK // 2
ROWS = 256
BF = jnp.bfloat16
F32 = jnp.float32


def rms_rows(row_block, gain_vec):
    values = row_block.astype(F32)
    scale = lax.rsqrt(jnp.mean(values * values, axis=-1, keepdims=True) + 1e-06)
    return (values * scale * gain_vec).astype(BF)


def even_odd(matrix):
    rows = matrix.shape[0]
    new = jnp.arange(DK, dtype=jnp.int32)
    old = jnp.where(new < HALF, 2 * new, 2 * (new - HALF) + 1)
    one_hot = (jnp.arange(DK, dtype=jnp.int32)[:, None] == old[None, :]).astype(BF)
    heads = matrix.reshape(rows * H, DK)
    return jnp.dot(heads, one_hot, preferred_element_type=F32).astype(BF).reshape(rows, H * DK)


def by_owner(matrix, width, share, mp_count):
    rows = matrix.shape[0]
    if share > 1:
        heads = jnp.repeat(matrix.reshape(rows, H, width), share, axis=1)
        return heads.transpose(1, 0, 2)
    return matrix.reshape(rows, mp_count, -1).transpose(1, 0, 2)


def ring_gather(block, count):
    order = [(i, (i + 1) % count) for i in range(count)]
    blocks = [block]
    for _ in range(count - 1):
        blocks.append(lax.ppermute(blocks[-1], "mp", order))
    return blocks


def in_order(blocks, index):
    count, rows = len(blocks), blocks[0].shape[0]
    whole = jnp.zeros((count * rows, blocks[0].shape[1]), blocks[0].dtype)
    for step, block in enumerate(blocks):
        whole = lax.dynamic_update_slice_in_dim(whole, block, (index - step) % count * rows, 0)
    return whole


def ring_sum(parts, index, count):
    rows = parts.shape[0] // count
    order = [(i, (i + 1) % count) for i in range(count)]

    def part(place):
        return lax.dynamic_slice_in_dim(parts, place % count * rows, rows, 0).astype(F32)

    total = part(index - 1)
    for step in range(count - 1):
        moved = lax.ppermute(total.astype(BF), "mp", order)
        total = moved.astype(F32) + part(index - 2 - step)
    return total


def retention_kernel(dims, scalars, x_ref, cos_ref, sin_ref, run_col, run_row, w_ref, wo_ref, out_ref, k_all, v_all):
    heads, share, wq, wv, wg = dims
    step = pl.program_id(0)
    x = x_ref[...]
    cos, sin = cos_ref[...], sin_ref[...]

    def turned(first):
        a, b = first[:, :HALF], first[:, HALF:]
        return a * cos - b * sin, b * cos + a * sin

    rows = pl.ds(pl.multiple_of(step * ROWS, ROWS), ROWS)
    queries = []
    for h in range(heads):
        q0, q1 = turned(jnp.dot(x, w_ref[:, h * DK : (h + 1) * DK], preferred_element_type=F32))
        queries.append((q0 * DK**-0.5, q1 * DK**-0.5))
        k0, k1 = turned(jnp.dot(x, w_ref[:, wq + h * DK : wq + (h + 1) * DK], preferred_element_type=F32))
        k_all[rows, h * DK : h * DK + HALF] = k0.astype(BF)
        k_all[rows, h * DK + HALF : (h + 1) * DK] = k1.astype(BF)
    v_all[rows, :] = jnp.dot(x, w_ref[:, 2 * wq : 2 * wq + wv], preferred_element_type=F32).astype(BF)
    gate = jnp.dot(x, w_ref[:, 2 * wq + wv :], preferred_element_type=F32).astype(BF).astype(F32)
    gate = gate / (1.0 + jnp.exp(-gate))
    place = step * ROWS + lax.broadcasted_iota(jnp.int32, (ROWS, 1), 0)
    gate = jnp.where(place < scalars[0], gate, 0.0)
    live = place < scalars[0]

    for now in range(SPAN // ROWS):

        @pl.when(step == now)
        def _():
            seen = (now + 1) * ROWS
            pieces = []
            for h in range(heads):
                q = jnp.concatenate([queries[h][0].astype(BF), queries[h][1].astype(BF)], axis=1)
                scores = lax.dot_general(
                    q, k_all[:seen, h * DK : (h + 1) * DK], (((1,), (1,)), ((), ())), preferred_element_type=F32
                )
                gap = run_col[:, h : h + 1] - run_row[h : h + 1, :seen]
                t = now * ROWS + lax.broadcasted_iota(jnp.int32, (ROWS, seen), 0)
                s = lax.broadcasted_iota(jnp.int32, (ROWS, seen), 1)
                weights = (scores * jnp.exp(jnp.where(t >= s, gap, -jnp.inf))).astype(BF)
                kept = jnp.dot(weights, v_all[:seen, h * DV : (h + 1) * DV], preferred_element_type=F32)
                mean = jnp.mean(kept, axis=-1, keepdims=True)
                spread = jnp.mean(kept * kept, axis=-1, keepdims=True) - mean * mean
                normed = (kept - mean) * lax.rsqrt(spread + 1e-05)
                if share > 1:
                    mine = normed[:, :wg]
                    for bit in range(1, share):
                        mine = jnp.where(scalars[1] == bit, normed[:, bit * wg : (bit + 1) * wg], mine)
                    normed = mine
                pieces.append(normed)
            whole = jnp.concatenate(pieces, axis=1) if heads > 1 else pieces[0]
            gated = jnp.where(live, gate * whole, 0.0).astype(BF)
            out_ref[...] = lax.dot_general(
                gated, wo_ref[...], (((1,), (1,)), ((), ())), preferred_element_type=F32
            ).astype(BF)


def retention(x, cos, sin, running, length, partner, w_in, w_out, heads, share):
    width = x.shape[1]
    wq, wv, wg = heads * DK, heads * DV, w_out.shape[1]
    dims = (heads, share, wq, wv, wg)
    scalars = jnp.stack([length, partner]).astype(jnp.int32)
    grid_spec = pltpu.PrefetchScalarGridSpec(
        num_scalar_prefetch=1,
        grid=(SPAN // ROWS,),
        in_specs=[
            pl.BlockSpec((ROWS, width), lambda i, _: (i, 0)),
            pl.BlockSpec((ROWS, HALF), lambda i, _: (i, 0)),
            pl.BlockSpec((ROWS, HALF), lambda i, _: (i, 0)),
            pl.BlockSpec((ROWS, heads), lambda i, _: (i, 0)),
            pl.BlockSpec((heads, SPAN), lambda i, _: (0, 0)),
            pl.BlockSpec(w_in.shape, lambda i, _: (0, 0), pipeline_mode=pl.Buffered(1)),
            pl.BlockSpec(w_out.shape, lambda i, _: (0, 0), pipeline_mode=pl.Buffered(1)),
        ],
        out_specs=pl.BlockSpec((ROWS, width), lambda i, _: (i, 0)),
        scratch_shapes=[pltpu.VMEM((SPAN, wq), BF), pltpu.VMEM((SPAN, wv), BF)],
    )
    return pl.pallas_call(
        lambda *refs: retention_kernel(dims, *refs),
        grid_spec=grid_spec,
        out_shape=jax.ShapeDtypeStruct((SPAN, width), BF),
        compiler_params=pltpu.CompilerParams(vmem_limit_bytes=48 * 2**20),
        cost_estimate=pl.CostEstimate(flops=20 * 10**9, bytes_accessed=26 * 10**6, transcendentals=2 * 10**6),
        name="retention",
    )(scalars, x, cos, sin, running, running.T, w_in, w_out)


def ffn_kernel(x_ref, w_ref, out_ref):
    width = out_ref.shape[1]
    x = x_ref[...]
    gate = jnp.dot(x, w_ref[:, :width], preferred_element_type=F32)
    up = jnp.dot(x, w_ref[:, width:], preferred_element_type=F32)
    out_ref[...] = (gate / (1.0 + jnp.exp(-gate)) * up).astype(BF)


def ffn(x, w):
    rows, width = x.shape
    out_width = w.shape[1] // 2
    return pl.pallas_call(
        ffn_kernel,
        grid=(rows // ROWS,),
        in_specs=[
            pl.BlockSpec((ROWS, width), lambda i: (i, 0)),
            pl.BlockSpec(w.shape, lambda i: (0, 0), pipeline_mode=pl.Buffered(1)),
        ],
        out_specs=pl.BlockSpec((ROWS, out_width), lambda i: (i, 0)),
        out_shape=jax.ShapeDtypeStruct((rows, out_width), BF),
        compiler_params=pltpu.CompilerParams(vmem_limit_bytes=40 * 2**20),
        cost_estimate=pl.CostEstimate(flops=2 * rows * width * w.shape[1], bytes_accessed=14 * 10**6, transcendentals=rows * out_width),
        name="ffn",
    )(x, w)


def per_device(
    tokens, norm_gain, mlp_gain, lengths, log_decay,
    query_master, key_master, value_master, swish_master, output_master, ffn_gate_master, ffn_up_master,
):
    mp_count = lax.axis_size("mp")
    mp_index = lax.axis_index("mp")
    share = max(1, mp_count // H)
    heads = max(1, H // mp_count)

    def handed_over(parts):
        block = jnp.concatenate(parts, axis=2)
        block = lax.all_to_all(block, "mp", split_axis=0, concat_axis=0, tiled=True)
        block = block.reshape(-1, block.shape[2])
        return lax.all_gather(block, "dp", axis=0, tiled=True)

    w_in = handed_over(
        [
            by_owner(even_odd(query_master.astype(BF)), DK, share, mp_count),
            by_owner(even_odd(key_master.astype(BF)), DK, share, mp_count),
            by_owner(value_master.astype(BF), DV, share, mp_count),
            by_owner(swish_master.astype(BF), DV, 1, mp_count),
        ]
    )
    w_out = handed_over([by_owner(output_master.astype(BF).T, DV, 1, mp_count)])
    w_ffn = handed_over(
        [by_owner(ffn_gate_master.astype(BF), DV, 1, mp_count), by_owner(ffn_up_master.astype(BF), DV, 1, mp_count)]
    )

    angles = jnp.arange(SPAN, dtype=jnp.int32).astype(F32)[:, None] * jnp.exp(
        (2 * jnp.arange(HALF, dtype=jnp.int32)).astype(F32) * (-math.log(10000.0) / DK)
    )
    cos, sin = jnp.cos(angles), jnp.sin(angles)
    first_head = mp_index // share * heads
    running = jnp.cumsum(lax.dynamic_slice_in_dim(log_decay, first_head, heads, 1), axis=0)

    normed_in = in_order(ring_gather(rms_rows(tokens, norm_gain), mp_count), mp_index)
    branch = retention(normed_in, cos, sin, running, lengths[0], mp_index % share, w_in, w_out, heads, share)
    residual = (tokens.astype(F32) + ring_sum(branch, mp_index, mp_count)).astype(BF)
    normed_mid = in_order(ring_gather(rms_rows(residual, mlp_gain), mp_count), mp_index)
    return residual, ffn(normed_mid, w_ffn)


def solution(mesh):
    rows, columns = P(("dp", "mp"), None), P(None, ("dp", "mp"))
    placed = (rows, P(), P(), P("dp"), P("dp", None), rows, rows, rows, rows, columns, rows, rows)
    return jax.shard_map(
        per_device, mesh=mesh, in_specs=placed, out_specs=(rows, P("dp", "mp")), check_vma=False
    )
```

time: 938 us -> 375 us (0.40)
  waiting for transfers between devices: 610 us -> 223 us
  local copies, waits for them, and re-layouts: 169 us -> 19.4 us
  blocking collectives: 0 us -> 60.3 us
  matrix products: 53.2 us -> 0.54 us
  Pallas kernels: 0 us -> 40 us
  other arithmetic: 48.7 us -> 11.4 us
  starting transfers between devices: 34.3 us -> 4.1 us
    all_to_all x7 -> x1, waiting for transfers between devices: 438 us -> 24.4 us  [handed_over(): block = lax.all_to_all(block, 'mp', split_axis=0, concat_axis=0, tiled=True)]
    ppermute x0 -> x9, waiting for transfers between devices: none -> 199 us  [the longest x6 132 us: ring_gather(): blocks.append(lax.ppermute(blocks[-1], 'mp', order))]
    reduce_scatter x1 -> x0, waiting for transfers between devices: 119 us -> none  [per_device(): lax.psum_scatter(lax.dot_general(gated, w_output, (((1,), (1,)), ((), ())...]
    all_to_all x0 -> x2, blocking collectives: none -> 60.3 us  [handed_over(): block = lax.all_to_all(block, 'mp', split_axis=0, concat_axis=0, tiled=True)]
    dot_general x5 -> x2, matrix products: 53.2 us -> 0.54 us  [even_odd(): jnp.dot(heads, one_hot, preferred_element_type=F32).astype(BF)]
    all_gather x9 -> x3, waiting for transfers between devices: 52.5 us -> 0.01 us  [handed_over(): return lax.all_gather(block, 'dp', axis=0, tiled=True)]
    all_gather x7 -> x0, local copies, waits for them, and re-layouts: 40.4 us -> none  [the longest x1 6.62 us: per_device(): lax.all_gather(m_swish, 'dp', axis=0, tiled=True)]
    pallas_call x0 -> x2, Pallas kernels: none -> 40 us  [the longest x1 29.8 us: retention(): pl.pallas_call(lambda *refs: retention_kernel(dims, *refs), grid_spec=gri...]
  transfers between devices with their start and end apart: 17 -> 13, of which waited for: 10 -> 10; matrix products, arithmetic and copies ran while one was open for 27% -> 6% of each run, Pallas kernels for 0% -> 8%
where the time goes in v1:
time: 375 us; the launch traced here: 374 us
  waiting for transfers between devices  223 us (59%)
  blocking collectives  60.3 us (16%)
  Pallas kernels  40 us (11%)
  local copies, waits for them, and re-layouts  19.4 us (5%)
  between operations  14.9 us (4%)
  other arithmetic  11.4 us (3%)
  starting transfers between devices  4.1 us (1%)
    ppermute x6, waiting for transfers between devices, ring_gather(): blocks.append(lax.ppermute(blocks[-1], 'mp', order))  132 us
    ppermute x3, waiting for transfers between devices, ring_sum(): moved = lax.ppermute(total.astype(BF), 'mp', order)  67.1 us
    all_to_all x2, blocking collectives, handed_over(): block = lax.all_to_all(block, 'mp', split_axis=0, concat_axis=0, tiled=True)  60.3 us
    pallas_call x1, Pallas kernels, retention(): pl.pallas_call(lambda *refs: retention_kernel(dims, *refs), grid_spec=gri...  29.8 us
    all_to_all x1, waiting for transfers between devices, handed_over(): block = lax.all_to_all(block, 'mp', split_axis=0, concat_axis=0, tiled=True)  24.4 us
    pallas_call x1, Pallas kernels, ffn(): pl.pallas_call(ffn_kernel, grid=(rows // ROWS,), in_specs=[pl.BlockSpec((...  10.2 us
    unnamed x37, local copies, waits for them, and re-layouts  8.75 us
  transfers between devices with their start and end apart: 13, of which 10 were waited for; matrix products, arithmetic and copies ran while one was open for 6% of the time, Pallas kernels for 8%

profile of v1, /device:TPU:0, one launch (start us, length us, event | category | flops | bytes accessed | tf_op | source)
XLA Modules:
  0.0 374.1 jit_solution(10930762309061759751)
XLA Ops:
  7.2 1.4 convert_element_type.107
  8.7 20.8 %all_to_all.15 = bf16[4,64,1024]{2,1,0:T(8,128)(2,1)} all-to-all(bf16[4,64,1024]{2,1,0:T(8,128)(2,1)S(1)} %bitcast.65), channel_id=1, replica_groups=mesh['dp'=8,'mp'=4] {'mp'}, dimensions={0} | all-to-all | bytes 1048576 | tf_op jit(solution)/shard_map/all_to_all | solution.py:197
  29.7 0.1 convert_element_type.105
  29.7 0.1 convert_element_type.106
  29.8 0.1 reshape.86
  30.0 0.3 fusion.7
  30.3 0.1 copy.20
  30.4 0.2 reshape_reshape.6
  30.6 1.1 convert_element_type.102
  31.7 0.1 reshape.87
  31.8 0.3 fusion.8
  32.1 0.1 copy.21
  32.3 0.2 reshape_reshape.7
  32.5 0.1 bitcast_bitcast_fusion.3
  32.6 0.1 pad_maximum_fusion
  32.8 39.5 %all_to_all.16 = bf16[4,64,3072]{2,1,0:T(8,128)(2,1)} all-to-all(bf16[4,64,3072]{2,1,0:T(8,128)(2,1)S(1)} %pad_maximum_fusion), channel_id=1, replica_groups=mesh['dp'=8,'mp'=4] {'mp'}, dimensions={0} | all-to-all | bytes 3145728 | tf_op jit(solution)/shard_map/all_to_all | solution.py:197
  72.3 0.1 convert_element_type.119
  72.3 0.1 convert_element_type.120
  72.4 0.1 bitcast_bitcast_fusion
  72.5 1.1 pad_maximum_fusion.1
  73.6 3.5 all-to-all-start.2
  77.2 0.3 fusion.3
  77.5 24.4 %all-to-all-done.2 = bf16[4,64,2048]{2,1,0:T(8,128)(2,1)S(1)} async-done(((bf16[4,64,2048]{2,1,0:T(8,128)(2,1)}), bf16[4,64,2048]{2,1,0:T(8,128)(2,1)S(1)}, u32[]{:S(2)}, u32[]{:S(2)}) %all-to-all-start.2) | async-done | bytes 1048608 | tf_op jit(solution)/shard_map/all_to_all | solution.py:197
  101.8 1.0 copy-done.8
  102.8 2.5 broadcast.85.clone
  105.3 1.4 constant_dynamic-update-slice_fusion.7
  106.7 25.9 %collective-permute-done = bf16[256,2048]{1,0:T(8,128)(2,1)S(1)} collective-permute-done((bf16[256,2048]{1,0:T(8,128)(2,1)S(1)}, bf16[256,2048]{1,0:T(8,128)(2,1)S(1)}, u32[]{:S(2)}, u32[]{:S(2)}) %collective-permute-start) | collective-permute-done | bytes 1048608 | tf_op jit(solution)/shard_map/ppermute | solution.py:47
  132.7 0.6 reduce-window.6
  133.3 0.2 slice_reduce_fusion
  133.4 0.2 reduce-window.9
  133.6 0.1 add_bitcast_fusion
  133.7 0.2 copy.27.refs_4_
  134.6 23.1 %collective-permute-done.1 = bf16[256,2048]{1,0:T(8,128)(2,1)} collective-permute-done((bf16[256,2048]{1,0:T(8,128)(2,1)S(1)}, bf16[256,2048]{1,0:T(8,128)(2,1)}, u32[]{:S(2)}, u32[]{:S(2)}) %collective-permute-start.1) | collective-permute-done | bytes 1048608 | tf_op jit(solution)/shard_map/ppermute | solution.py:47
  157.7 0.1 pad_add_fusion.refs_0_
  157.8 1.9 multiply_sine_fusion
  159.7 2.3 constant_dynamic-update-slice_fusion.6
  162.0 2.3 constant_dynamic-update-slice_fusion.5
  164.4 17.6 %collective-permute-done.2 = bf16[256,2048]{1,0:T(8,128)(2,1)S(1)} collective-permute-done((bf16[256,2048]{1,0:T(8,128)(2,1)}, bf16[256,2048]{1,0:T(8,128)(2,1)S(1)}, u32[]{:S(2)}, u32[]{:S(2)}) %collective-permute-start.2) | collective-permute-done | bytes 1048608 | tf_op jit(solution)/shard_map/ppermute | solution.py:47
  182.0 1.1 constant_dynamic-update-slice_fusion.4.refs_1_
  183.1 29.8 %retention.1 = bf16[1024,2048]{1,0:T(8,128)(2,1)S(1)} custom-call(s32[2]{0:T(128)S(1)} %pad_add_fusion.refs_0_, bf16[1024,2048]{1,0:T(8,128)(2,1)} %constant_dynamic-update-slice_fusion.4.refs_1_, f32[1024,128]{1,0:T(8,128)S(1)} %get-tuple-element.11.refs_2_, f32[1024,128]{1,0:T(8,128)S(1)} %get-tuple-element.10.refs_3_, f32[1024,2]{1,0:T(8,128)S(1)} %copy.27.refs_4_, ...), custom_call_target="tpu_custom_call" | custom-call | flops 20000000000 | bytes 26000000 | tf_op jit(solution)/shard_map/retention/pallas_call | solution.py:150
  212.9 0.1 constant_dynamic-slice_fusion
  213.0 0.1 collective-permute-start.3
  213.0 23.1 %collective-permute-done.3 = bf16[256,2048]{1,0:T(8,128)(2,1)S(1)} collective-permute-done((bf16[256,2048]{1,0:T(8,128)(2,1)S(1)}, bf16[256,2048]{1,0:T(8,128)(2,1)S(1)}, u32[]{:S(2)}, u32[]{:S(2)}) %collective-permute-start.3) | collective-permute-done | bytes 1048608 | tf_op jit(solution)/shard_map/ppermute | solution.py:68
  236.2 0.4 add_convert_fusion.1
  236.6 0.1 collective-permute-start.4
  236.6 22.6 %collective-permute-done.4 = bf16[256,2048]{1,0:T(8,128)(2,1)S(1)} collective-permute-done((bf16[256,2048]{1,0:T(8,128)(2,1)S(1)}, bf16[256,2048]{1,0:T(8,128)(2,1)S(1)}, u32[]{:S(2)}, u32[]{:S(2)}) %collective-permute-start.4) | collective-permute-done | bytes 1048608 | tf_op jit(solution)/shard_map/ppermute | solution.py:68
  259.2 0.4 add_convert_fusion
  259.7 0.3 collective-permute-start.5
  260.0 21.3 %collective-permute-done.5 = bf16[256,2048]{1,0:T(8,128)(2,1)S(1)} collective-permute-done((bf16[256,2048]{1,0:T(8,128)(2,1)S(1)}, bf16[256,2048]{1,0:T(8,128)(2,1)S(1)}, u32[]{:S(2)}, u32[]{:S(2)}) %collective-permute-start.5) | collective-permute-done | bytes 1048608 | tf_op jit(solution)/shard_map/ppermute | solution.py:68
  281.3 1.9 fusion
  283.2 0.5 broadcast.85
  283.7 0.2 copy-done.16
  283.9 0.3 constant_dynamic-update-slice_fusion.3
  284.2 0.1 collective-permute-start.6
  284.3 23.3 %collective-permute-done.6 = bf16[256,2048]{1,0:T(8,128)(2,1)S(1)} collective-permute-done((bf16[256,2048]{1,0:T(8,128)(2,1)S(1)}, bf16[256,2048]{1,0:T(8,128)(2,1)S(1)}, u32[]{:S(2)}, u32[]{:S(2)}) %collective-permute-start.6) | collective-permute-done | bytes 1048608 | tf_op jit(solution)/shard_map/ppermute | solution.py:47
  307.6 23.3 %collective-permute-done.7 = bf16[256,2048]{1,0:T(8,128)(2,1)S(1)} collective-permute-done((bf16[256,2048]{1,0:T(8,128)(2,1)S(1)}, bf16[256,2048]{1,0:T(8,128)(2,1)S(1)}, u32[]{:S(2)}, u32[]{:S(2)}) %collective-permute-start.7) | collective-permute-done | bytes 1048608 | tf_op jit(solution)/shard_map/ppermute | solution.py:47
  330.9 0.1 constant_dynamic-update-slice_fusion.2
  331.0 0.1 constant_dynamic-update-slice_fusion.1
  331.2 18.5 %collective-permute-done.8 = bf16[256,2048]{1,0:T(8,128)(2,1)S(1)} collective-permute-done((bf16[256,2048]{1,0:T(8,128)(2,1)S(1)}, bf16[256,2048]{1,0:T(8,128)(2,1)S(1)}, u32[]{:S(2)}, u32[]{:S(2)}) %collective-permute-start.8) | collective-permute-done | bytes 1048608 | tf_op jit(solution)/shard_map/ppermute | solution.py:47
  349.7 0.1 constant_dynamic-update-slice_fusion.x_ref
  349.8 1.9 copy-done.3
  351.8 2.2 copy-done.4
  353.9 3.4 copy-done.5
  357.3 10.2 %ffn.1 = bf16[1024,1024]{1,0:T(8,128)(2,1)} custom-call(bf16[1024,2048]{1,0:T(8,128)(2,1)S(1)} %copy-done.4, bf16[2048,2048]{1,0:T(8,128)(2,1)S(1)} %copy-done.5), custom_call_target="tpu_custom_call" | custom-call | flops 8589934592 | bytes 14000000 | tf_op jit(solution)/shard_map/ffn/pallas_call | solution.py:171
  (55 shorter events, 0.5 us)
Async XLA Ops:
  7.2 125.5 %copy-start = (f32[1024,8]{0,1:T(8,128)S(1)}, f32[1024,8]{0,1:T(8,128)}, u32[]{:S(2)}) copy-start(f32[1024,8]{0,1:T(8,128)} %param.16) | copy-start | bytes 98308
  7.2 22.5 %copy-start.10 = (f32[64,4096]{1,0:T(8,128)S(1)}, f32[64,4096]{1,0:T(8,128)}, u32[]{:S(2)}) copy-start(f32[64,4096]{1,0:T(8,128)} %param.19) | copy-start | bytes 3145732
  7.2 22.5 %copy-start.11 = (f32[64,4096]{1,0:T(8,128)S(1)}, f32[64,4096]{1,0:T(8,128)}, u32[]{:S(2)}) copy-start(f32[64,4096]{1,0:T(8,128)} %param.20) | copy-start | bytes 3145732
  7.2 175.9 %all-gather.6.cloned.1.call-start = ((), (), s32[]{:S(2)}) async-start(), calls=%async_computation.4 | async-start | bytes 4718592 | tf_op jit(solution)/shard_map/all_gather | solution.py:199
  8.7 21.1 %copy-start.14 = (f32[64,2048]{1,0:T(8,128)S(1)}, f32[64,2048]{1,0:T(8,128)}, u32[]{:S(2)}) copy-start(f32[64,2048]{1,0:T(8,128)} %param.17) | copy-start | bytes 1572868
  29.6 153.5 %all-gather.4.cloned.1.call-start = ((), (), s32[]{:S(2)}) async-start(), calls=%async_computation.3 | async-start | bytes 14155776 | tf_op jit(solution)/shard_map/all_gather | solution.py:199
  32.7 39.5 %copy-start.12 = (f32[64,4096]{1,0:T(8,128)S(1)}, f32[64,4096]{1,0:T(8,128)}, u32[]{:S(2)}) copy-start(f32[64,4096]{1,0:T(8,128)} %param.22) | copy-start | bytes 3145732
  32.7 39.6 %copy-start.13 = (f32[64,4096]{1,0:T(8,128)S(1)}, f32[64,4096]{1,0:T(8,128)}, u32[]{:S(2)}) copy-start(f32[64,4096]{1,0:T(8,128)} %param.23) | copy-start | bytes 3145732
  72.4 4.8 %copy-start.6 = (bf16[256,2048]{1,0:T(8,128)(2,1)S(1)}, bf16[256,2048]{1,0:T(8,128)(2,1)}, u32[]{:S(2)}) copy-start(bf16[256,2048]{1,0:T(8,128)(2,1)} %param.12) | copy-start | bytes 3145732
  73.6 28.3 %all-to-all-start.2 = ((bf16[4,64,2048]{2,1,0:T(8,128)(2,1)}), bf16[4,64,2048]{2,1,0:T(8,128)(2,1)S(1)}, u32[]{:S(2)}, u32[]{:S(2)}) async-start(bf16[4,64,2048]{2,1,0:T(8,128)(2,1)} %pad_maximum_fusion.1), calls=%async_computation.2 | async-start | bytes 2097152 | tf_op jit(solution)/shard_map/all_to_all | solution.py:197
  77.1 274.7 %all-gather.8.cloned.1.call-start = ((), (), s32[]{:S(2)}) async-start(), calls=%async_computation.5 | async-start | bytes 9437184 | tf_op jit(solution)/shard_map/all_gather | solution.py:199
  77.2 28.2 %copy-start.15 = (f32[2048]{0:T(1024)S(1)}, f32[2048]{0:T(1024)}, u32[]{:S(2)}) copy-start(f32[2048]{0:T(1024)} %param.13) | copy-start | bytes 24580
  101.8 1.0 copy-start.8
  106.7 25.9 %collective-permute-start = (bf16[256,2048]{1,0:T(8,128)(2,1)S(1)}, bf16[256,2048]{1,0:T(8,128)(2,1)S(1)}, u32[]{:S(2)}, u32[]{:S(2)}) collective-permute-start(bf16[256,2048]{1,0:T(8,128)(2,1)S(1)} %get-tuple-element.7), channel_id=1, source_target_pairs={{0,1},{1,2},{2,3},{3,0},{4,5},{5,6},{6,7},{7,4},{8,9},{9,10},{10,1... | collective-permute-start | bytes 3145736 | tf_op jit(solution)/shard_map/ppermute | solution.py:47
  132.6 25.2 %copy-start.9 = (bf16[256,2048]{1,0:T(8,128)(2,1)}, bf16[256,2048]{1,0:T(8,128)(2,1)S(1)}, u32[]{:S(2)}) copy-start(bf16[256,2048]{1,0:T(8,128)(2,1)S(1)} %collective-permute-done) | copy-start | bytes 3145732
  132.6 25.1 %collective-permute-start.1 = (bf16[256,2048]{1,0:T(8,128)(2,1)S(1)}, bf16[256,2048]{1,0:T(8,128)(2,1)}, u32[]{:S(2)}, u32[]{:S(2)}) collective-permute-start(bf16[256,2048]{1,0:T(8,128)(2,1)S(1)} %collective-permute-done), channel_id=1, source_target_pairs={{0,1},{1,2},{2,3},{3,0},{4,5},{5,6},{6,7},{7,4},{8,9},{9,10},{10,1... | collective-permute-start | bytes 3145736 | tf_op jit(solution)/shard_map/ppermute | solution.py:47
  157.7 24.3 %collective-permute-start.2 = (bf16[256,2048]{1,0:T(8,128)(2,1)}, bf16[256,2048]{1,0:T(8,128)(2,1)S(1)}, u32[]{:S(2)}, u32[]{:S(2)}) collective-permute-start(bf16[256,2048]{1,0:T(8,128)(2,1)} %collective-permute-done.1), channel_id=1, source_target_pairs={{0,1},{1,2},{2,3},{3,0},{4,5},{5,6},{6,7},{7,4},{8,9},{9,10},{10,1... | collective-permute-start | bytes 3145736 | tf_op jit(solution)/shard_map/ppermute | solution.py:47
  212.9 46.8 %copy-start.2 = (bf16[1024,2048]{1,0:T(8,128)(2,1)}, bf16[1024,2048]{1,0:T(8,128)(2,1)S(1)}, u32[]{:S(2)}) copy-start(bf16[1024,2048]{1,0:T(8,128)(2,1)S(1)} %retention.1) | copy-start | bytes 12582916
  213.0 23.2 %collective-permute-start.3 = (bf16[256,2048]{1,0:T(8,128)(2,1)S(1)}, bf16[256,2048]{1,0:T(8,128)(2,1)S(1)}, u32[]{:S(2)}, u32[]{:S(2)}) collective-permute-start(bf16[256,2048]{1,0:T(8,128)(2,1)S(1)} %constant_dynamic-slice_fusion), channel_id=1, source_target_pairs={{0,1},{1,2},{2,3},{3,0},{4,5},{5,6},{6,7},{7,4},{8,9},{9,10},{10,1... | collective-permute-start | bytes 3145736 | tf_op jit(solution)/shard_map/ppermute | solution.py:68
  236.6 22.7 %collective-permute-start.4 = (bf16[256,2048]{1,0:T(8,128)(2,1)S(1)}, bf16[256,2048]{1,0:T(8,128)(2,1)S(1)}, u32[]{:S(2)}, u32[]{:S(2)}) collective-permute-start(bf16[256,2048]{1,0:T(8,128)(2,1)S(1)} %add_convert_fusion.1), channel_id=1, source_target_pairs={{0,1},{1,2},{2,3},{3,0},{4,5},{5,6},{6,7},{7,4},{8,9},{9,10},{10,1... | collective-permute-start | bytes 3145736 | tf_op jit(solution)/shard_map/ppermute | solution.py:68
  259.7 21.6 %collective-permute-start.5 = (bf16[256,2048]{1,0:T(8,128)(2,1)S(1)}, bf16[256,2048]{1,0:T(8,128)(2,1)S(1)}, u32[]{:S(2)}, u32[]{:S(2)}) collective-permute-start(bf16[256,2048]{1,0:T(8,128)(2,1)S(1)} %add_convert_fusion), channel_id=1, source_target_pairs={{0,1},{1,2},{2,3},{3,0},{4,5},{5,6},{6,7},{7,4},{8,9},{9,10},{10,1... | collective-permute-start | bytes 3145736 | tf_op jit(solution)/shard_map/ppermute | solution.py:68
  283.2 1.0 copy-start.7
  283.2 0.7 copy-start.16
  284.2 23.4 %collective-permute-start.6 = (bf16[256,2048]{1,0:T(8,128)(2,1)S(1)}, bf16[256,2048]{1,0:T(8,128)(2,1)S(1)}, u32[]{:S(2)}, u32[]{:S(2)}) collective-permute-start(bf16[256,2048]{1,0:T(8,128)(2,1)S(1)} %get-tuple-element.3), channel_id=1, source_target_pairs={{0,1},{1,2},{2,3},{3,0},{4,5},{5,6},{6,7},{7,4},{8,9},{9,10},{10,1... | collective-permute-start | bytes 3145736 | tf_op jit(solution)/shard_map/ppermute | solution.py:47
  307.6 23.3 %collective-permute-start.7 = (bf16[256,2048]{1,0:T(8,128)(2,1)S(1)}, bf16[256,2048]{1,0:T(8,128)(2,1)S(1)}, u32[]{:S(2)}, u32[]{:S(2)}) collective-permute-start(bf16[256,2048]{1,0:T(8,128)(2,1)S(1)} %collective-permute-done.6), channel_id=1, source_target_pairs={{0,1},{1,2},{2,3},{3,0},{4,5},{5,6},{6,7},{7,4},{8,9},{9,10},{10,1... | collective-permute-start | bytes 3145736 | tf_op jit(solution)/shard_map/ppermute | solution.py:47
  330.9 18.7 %collective-permute-start.8 = (bf16[256,2048]{1,0:T(8,128)(2,1)S(1)}, bf16[256,2048]{1,0:T(8,128)(2,1)S(1)}, u32[]{:S(2)}, u32[]{:S(2)}) collective-permute-start(bf16[256,2048]{1,0:T(8,128)(2,1)S(1)} %collective-permute-done.7), channel_id=1, source_target_pairs={{0,1},{1,2},{2,3},{3,0},{4,5},{5,6},{6,7},{7,4},{8,9},{9,10},{10,1... | collective-permute-start | bytes 3145736 | tf_op jit(solution)/shard_map/ppermute | solution.py:47
  349.8 2.0 copy-start.3
  351.8 2.2 copy-start.4
  353.9 3.4 copy-start.5
  357.3 10.2 %copy-start.1 = (f32[1024,8]{0,1:T(8,128)S(1)}, f32[1024,8]{0,1:T(8,128)}, u32[]{:S(2)}) copy-start(f32[1024,8]{0,1:T(8,128)} %param.16) | copy-start | bytes 98308
Sparse Core Ops, SparseCore 0:
  29.7 35.8 all-gather.5
  72.4 71.2 all-gather.3
  146.1 54.3 all-gather.7

commit v2 on v1

v2 whole, which is shorter than its diff:
```python
import math

import jax
import jax.numpy as jnp
from jax import lax
from jax.experimental import pallas as pl
from jax.experimental.pallas import tpu as pltpu
from jax.sharding import PartitionSpec as P

H = 8
DK = 256
DV = 512
SPAN = 1024
HALF = DK // 2
ROWS = 256
BF = jnp.bfloat16
F32 = jnp.float32


def rms_rows(row_block, gain_vec):
    values = row_block.astype(F32)
    scale = lax.rsqrt(jnp.mean(values * values, axis=-1, keepdims=True) + 1e-06)
    return (values * scale * gain_vec).astype(BF)


def even_odd(matrix):
    rows = matrix.shape[0]
    new = jnp.arange(DK, dtype=jnp.int32)
    old = jnp.where(new < HALF, 2 * new, 2 * (new - HALF) + 1)
    one_hot = (jnp.arange(DK, dtype=jnp.int32)[:, None] == old[None, :]).astype(BF)
    heads = matrix.reshape(rows * H, DK)
    return jnp.dot(heads, one_hot, preferred_element_type=F32).astype(BF).reshape(rows, H * DK)


def by_owner(matrix, width, share, mp_count):
    rows = matrix.shape[0]
    if share > 1:
        heads = jnp.repeat(matrix.reshape(rows, H, width), share, axis=1)
        return heads.transpose(1, 0, 2)
    return matrix.reshape(rows, mp_count, -1).transpose(1, 0, 2)


def ring_gather(block, count):
    order = [(i, (i + 1) % count) for i in range(count)]
    blocks = [block]
    for _ in range(count - 1):
        blocks.append(lax.ppermute(blocks[-1], "mp", order))
    return blocks


def in_order(blocks, index):
    count, rows = len(blocks), blocks[0].shape[0]
    whole = jnp.zeros((count * rows, blocks[0].shape[1]), blocks[0].dtype)
    for step, block in enumerate(blocks):
        whole = lax.dynamic_update_slice_in_dim(whole, block, (index - step) % count * rows, 0)
    return whole


def exchanged(block, index, count):
    pieces = []
    for shift in range(count):
        piece = lax.dynamic_index_in_dim(block, (index + shift) % count, 0, keepdims=False)
        if shift:
            piece = lax.ppermute(piece, "mp", [(i, (i + shift) % count) for i in range(count)])
        pieces.append(piece)
    return pieces


def ring_sum(parts, index, count):
    rows = parts.shape[0] // count
    order = [(i, (i + 1) % count) for i in range(count)]

    def part(place):
        return lax.dynamic_slice_in_dim(parts, place % count * rows, rows, 0).astype(F32)

    total = part(index - 1)
    for step in range(count - 1):
        moved = lax.ppermute(total.astype(BF), "mp", order)
        total = moved.astype(F32) + part(index - 2 - step)
    return total


def project_kernel(heads, scalars, x_ref, gain_ref, cos_ref, sin_ref, w_ref, *refs):
    normed_ref, out_ref = refs[-2:]
    wq = heads * DK
    x = rms_rows(x_ref[...], gain_ref[...])
    normed_ref[...] = x
    cos, sin = cos_ref[...], sin_ref[...]
    for h in range(2 * heads):
        low = h * DK
        both = jnp.dot(x, w_ref[:, low : low + DK], preferred_element_type=F32)
        a, b = both[:, :HALF], both[:, HALF:]
        scale = DK**-0.5 if h < heads else 1.0
        out_ref[:, low : low + HALF] = ((a * cos - b * sin) * scale).astype(BF)
        out_ref[:, low + HALF : low + DK] = ((b * cos + a * sin) * scale).astype(BF)
    out_ref[:, 2 * wq :] = jnp.dot(x, w_ref[:, 2 * wq :], preferred_element_type=F32).astype(BF)


def project(x, place, gain, cos, sin, w, heads, held):
    rows, width = x.shape
    out_width = w.shape[1]
    extra = [] if held is None else list(held)
    grid_spec = pltpu.PrefetchScalarGridSpec(
        num_scalar_prefetch=1,
        grid=(1,),
        in_specs=[
            pl.BlockSpec((rows, width), lambda i, s: (0, 0)),
            pl.BlockSpec((1, width), lambda i, s: (0, 0)),
            pl.BlockSpec((rows, HALF), lambda i, s: (s[0], 0)),
            pl.BlockSpec((rows, HALF), lambda i, s: (s[0], 0)),
            pl.BlockSpec(w.shape, lambda i, s: (0, 0)),
        ]
        + [pl.BlockSpec(memory_space=pl.ANY)] * len(extra),
        out_specs=[
            pl.BlockSpec((rows, width), lambda i, s: (s[0], 0)),
            pl.BlockSpec((rows, out_width), lambda i, s: (s[0], 0)),
        ],
    )
    return pl.pallas_call(
        lambda *refs: project_kernel(heads, *refs),
        grid_spec=grid_spec,
        out_shape=[jax.ShapeDtypeStruct((SPAN, width), BF), jax.ShapeDtypeStruct((SPAN, out_width), BF)],
        input_output_aliases={6: 0, 7: 1} if extra else {},
        compiler_params=pltpu.CompilerParams(vmem_limit_bytes=48 * 2**20),
        cost_estimate=pl.CostEstimate(
            flops=2 * rows * width * out_width, bytes_accessed=2 * (w.size + rows * (width + out_width)), transcendentals=0
        ),
        name="project",
    )(place.reshape(1).astype(jnp.int32), x, gain.reshape(1, -1), cos, sin, w, *extra)


def retention_kernel(dims, scalars, x_ref, run_col, run_row, qkv_ref, w_ref, out_ref):
    heads, share, wq, wv, wg = dims
    step = pl.program_id(0)
    gate = jnp.dot(x_ref[...], w_ref[:, :wg], preferred_element_type=F32).astype(BF).astype(F32)
    gate = gate / (1.0 + jnp.exp(-gate))
    live = step * ROWS + lax.broadcasted_iota(jnp.int32, (ROWS, 1), 0) < scalars[0]

    for now in range(SPAN // ROWS):

        @pl.when(step == now)
        def _():
            seen = (now + 1) * ROWS
            pieces = []
            for h in range(heads):
                scores = lax.dot_general(
                    qkv_ref[now * ROWS : seen, h * DK : (h + 1) * DK],
                    qkv_ref[:seen, wq + h * DK : wq + (h + 1) * DK],
                    (((1,), (1,)), ((), ())),
                    preferred_element_type=F32,
                )
                gap = run_col[:, h : h + 1] - run_row[h : h + 1, :seen]
                t = now * ROWS + lax.broadcasted_iota(jnp.int32, (ROWS, seen), 0)
                s = lax.broadcasted_iota(jnp.int32, (ROWS, seen), 1)
                weights = (scores * jnp.exp(jnp.where(t >= s, gap, -jnp.inf))).astype(BF)
                values = qkv_ref[:seen, 2 * wq + h * DV : 2 * wq + (h + 1) * DV]
                kept = jnp.dot(weights, values, preferred_element_type=F32)
                mean = jnp.mean(kept, axis=-1, keepdims=True)
                spread = jnp.mean(kept * kept, axis=-1, keepdims=True) - mean * mean
                normed = (kept - mean) * lax.rsqrt(spread + 1e-05)
                if share > 1:
                    mine = normed[:, :wg]
                    for bit in range(1, share):
                        mine = jnp.where(scalars[1] == bit, normed[:, bit * wg : (bit + 1) * wg], mine)
                    normed = mine
                pieces.append(normed)
            whole = jnp.concatenate(pieces, axis=1) if heads > 1 else pieces[0]
            gated = jnp.where(live, gate * whole, 0.0).astype(BF)
            out_ref[...] = lax.dot_general(
                gated, w_ref[:, wg:], (((1,), (1,)), ((), ())), preferred_element_type=F32
            ).astype(BF)


def retention(x, running, length, partner, qkv, w, heads, share):
    width = x.shape[1]
    wq, wv, wg = heads * DK, heads * DV, w.shape[1] // 2
    dims = (heads, share, wq, wv, wg)
    scalars = jnp.stack([length, partner]).astype(jnp.int32)
    grid_spec = pltpu.PrefetchScalarGridSpec(
        num_scalar_prefetch=1,
        grid=(SPAN // ROWS,),
        in_specs=[
            pl.BlockSpec((ROWS, width), lambda i, _: (i, 0)),
            pl.BlockSpec((ROWS, heads), lambda i, _: (i, 0)),
            pl.BlockSpec((heads, SPAN), lambda i, _: (0, 0)),
            pl.BlockSpec(qkv.shape, lambda i, _: (0, 0), pipeline_mode=pl.Buffered(1)),
            pl.BlockSpec(w.shape, lambda i, _: (0, 0), pipeline_mode=pl.Buffered(1)),
        ],
        out_specs=pl.BlockSpec((ROWS, width), lambda i, _: (i, 0)),
    )
    return pl.pallas_call(
        lambda *refs: retention_kernel(dims, *refs),
        grid_spec=grid_spec,
        out_shape=jax.ShapeDtypeStruct((SPAN, width), BF),
        compiler_params=pltpu.CompilerParams(vmem_limit_bytes=48 * 2**20),
        cost_estimate=pl.CostEstimate(flops=12 * 10**9, bytes_accessed=20 * 10**6, transcendentals=2 * 10**6),
        name="retention",
    )(scalars, x, running, running.T, qkv, w)


def ffn_kernel(scalars, x_ref, w_ref, *refs):
    out_ref = refs[-1]
    width = out_ref.shape[1]
    x = x_ref[...]
    gate = jnp.dot(x, w_ref[:, :width], preferred_element_type=F32)
    up = jnp.dot(x, w_ref[:, width:], preferred_element_type=F32)
    out_ref[...] = (gate / (1.0 + jnp.exp(-gate)) * up).astype(BF)


def ffn(x, place, w, held):
    rows, width = x.shape
    out_width = w.shape[1] // 2
    extra = [] if held is None else [held]
    grid_spec = pltpu.PrefetchScalarGridSpec(
        num_scalar_prefetch=1,
        grid=(1,),
        in_specs=[pl.BlockSpec((rows, width), lambda i, s: (0, 0)), pl.BlockSpec(w.shape, lambda i, s: (0, 0))]
        + [pl.BlockSpec(memory_space=pl.ANY)] * len(extra),
        out_specs=pl.BlockSpec((rows, out_width), lambda i, s: (s[0], 0)),
    )
    return pl.pallas_call(
        ffn_kernel,
        grid_spec=grid_spec,
        out_shape=jax.ShapeDtypeStruct((SPAN, out_width), BF),
        input_output_aliases={3: 0} if extra else {},
        compiler_params=pltpu.CompilerParams(vmem_limit_bytes=40 * 2**20),
        cost_estimate=pl.CostEstimate(
            flops=2 * rows * width * w.shape[1], bytes_accessed=2 * w.size, transcendentals=rows * out_width
        ),
        name="ffn",
    )(place.reshape(1).astype(jnp.int32), x, w, *extra)


def per_device(
    tokens, norm_gain, mlp_gain, lengths, log_decay,
    query_master, key_master, value_master, swish_master, output_master, ffn_gate_master, ffn_up_master,
):
    mp_count = lax.axis_size("mp")
    mp_index = lax.axis_index("mp")
    share = max(1, mp_count // H)
    heads = max(1, H // mp_count)

    def at_owner(parts):
        block = jnp.concatenate(parts, axis=2)
        block = lax.all_to_all(block, "mp", split_axis=0, concat_axis=0, tiled=True)
        return block.reshape(-1, block.shape[2])

    angles = jnp.arange(SPAN, dtype=jnp.int32).astype(F32)[:, None] * jnp.exp(
        (2 * jnp.arange(HALF, dtype=jnp.int32)).astype(F32) * (-math.log(10000.0) / DK)
    )
    cos, sin = jnp.cos(angles), jnp.sin(angles)
    first_head = mp_index // share * heads
    running = jnp.cumsum(lax.dynamic_slice_in_dim(log_decay, first_head, heads, 1), axis=0)

    qkv_rows = at_owner(
        [
            by_owner(even_odd(query_master.astype(BF)), DK, share, mp_count),
            by_owner(even_odd(key_master.astype(BF)), DK, share, mp_count),
            by_owner(value_master.astype(BF), DV, share, mp_count),
        ]
    )
    w_qkv = lax.all_gather(qkv_rows, "dp", axis=0, tiled=True)
    swish, output, qkv_rows = lax.optimization_barrier((swish_master, output_master, qkv_rows))
    gate_out_rows = at_owner(
        [by_owner(swish.astype(BF), DV, 1, mp_count), by_owner(output.astype(BF).T, DV, 1, mp_count)]
    )
    w_gate_out = lax.all_gather(gate_out_rows, "dp", axis=0, tiled=True)

    order = [(i, (i + 1) % mp_count) for i in range(mp_count)]
    moving, _ = lax.optimization_barrier((tokens, gate_out_rows))
    blocks, qkv = [moving], None
    for step in range(mp_count):
        if step < mp_count - 1:
            arriving = lax.ppermute(moving, "mp", order)
            blocks.append(arriving)
        if step > 0:
            qkv = project(blocks[step - 1], (mp_index - step + 1) % mp_count, norm_gain, cos, sin, w_qkv, heads, qkv)
        if step < mp_count - 1:
            moving = arriving
            if step > 0:
                moving, qkv = lax.optimization_barrier((moving, qkv))
    qkv = project(blocks[-1], (mp_index + 1) % mp_count, norm_gain, cos, sin, w_qkv, heads, qkv)
    ffn_parts, qkv = lax.optimization_barrier(((ffn_gate_master, ffn_up_master), qkv))
    ffn_pieces = exchanged(
        jnp.concatenate([by_owner(m.astype(BF), DV, 1, mp_count) for m in ffn_parts], axis=2), mp_index, mp_count
    )
    branch = retention(qkv[0], running, lengths[0], mp_index % share, qkv[1], w_gate_out, heads, share)
    ffn_pieces, branch = lax.optimization_barrier((ffn_pieces, branch))
    w_ffn = lax.all_gather(in_order(ffn_pieces, mp_index), "dp", axis=0, tiled=True)
    residual = (tokens.astype(F32) + ring_sum(branch, mp_index, mp_count)).astype(BF)
    moving = rms_rows(residual, mlp_gain)
    hidden = None
    for step in range(mp_count):
        block = moving
        if step < mp_count - 1:
            arriving = lax.ppermute(moving, "mp", order)
        hidden = ffn(block, (mp_index - step) % mp_count, w_ffn, hidden)
        if step < mp_count - 1:
            moving, hidden = lax.optimization_barrier((arriving, hidden))
    return residual, hidden


def solution(mesh):
    rows, columns = P(("dp", "mp"), None), P(None, ("dp", "mp"))
    placed = (rows, P(), P(), P("dp"), P("dp", None), rows, rows, rows, rows, columns, rows, rows)
    return jax.shard_map(
        per_device, mesh=mesh, in_specs=placed, out_specs=(rows, P("dp", "mp")), check_vma=False
    )
```

time: 375 us -> 335 us (0.89)
  waiting for transfers between devices: 223 us -> 168 us
  Pallas kernels: 40 us -> 62.3 us
  local copies, waits for them, and re-layouts: 19.4 us -> 12.7 us
    pallas_call x1 -> x8, Pallas kernels: 10.2 us -> 42.9 us  [the longest x4 30.3 us: project(): pl.pallas_call(lambda *refs: project_kernel(heads, *refs), grid_spec=grid...]
    ppermute x6 -> x9, waiting for transfers between devices: 132 us -> 105 us  [the longest x6 105 us: per_device(): arriving = lax.ppermute(moving, 'mp', order)]
    all_to_all x1 -> x0, waiting for transfers between devices: 24.4 us -> none  [handed_over(): block = lax.all_to_all(block, 'mp', split_axis=0, concat_axis=0, tiled=True)]
    pallas_call x1, Pallas kernels: 29.8 us -> 19.4 us  [retention(): pl.pallas_call(lambda *refs: retention_kernel(dims, *refs), grid_spec=gri...]
    dynamic_update_slice x6 -> x4, local copies, waits for them, and re-layouts: 6.03 us -> 0.1 us  [in_order(): lax.dynamic_update_slice_in_dim(whole, block, (index - step) % count * ro...]
    ppermute x6 -> x9, starting transfers between devices: 0.07 us -> 4.47 us  [the longest x3 3.87 us: exchanged(): lax.ppermute(piece, 'mp', [(i, (i + shift) % count) for i in range(count)])]
    ppermute x3, waiting for transfers between devices: 67.1 us -> 63.2 us  [ring_sum(): moved = lax.ppermute(total.astype(BF), 'mp', order)]
  transfers between devices with their start and end apart: 13 -> 15, of which waited for: 10 -> 9; matrix products, arithmetic and copies ran while one was open for 6% -> 3% of each run, Pallas kernels for 8% -> 18%
where the time goes in v2:
time: 335 us; the launch traced here: 334 us
  waiting for transfers between devices  168 us (50%)
  Pallas kernels  62.3 us (19%)
  blocking collectives  60.2 us (18%)
  between operations  15 us (4%)
  local copies, waits for them, and re-layouts  12.7 us (4%)
  other arithmetic  10.3 us (3%)
  starting transfers between devices  5.33 us (2%)
    ppermute x6, waiting for transfers between devices, per_device(): arriving = lax.ppermute(moving, 'mp', order)  105 us
    ppermute x3, waiting for transfers between devices, ring_sum(): moved = lax.ppermute(total.astype(BF), 'mp', order)  63.2 us
    all_to_all x2, blocking collectives, at_owner(): block = lax.all_to_all(block, 'mp', split_axis=0, concat_axis=0, tiled=True)  60.2 us
    pallas_call x4, Pallas kernels, project(): pl.pallas_call(lambda *refs: project_kernel(heads, *refs), grid_spec=grid...  30.3 us
    pallas_call x1, Pallas kernels, retention(): pl.pallas_call(lambda *refs: retention_kernel(dims, *refs), grid_spec=gri...  19.4 us
    pallas_call x4, Pallas kernels, ffn(): pl.pallas_call(ffn_kernel, grid_spec=grid_spec, out_shape=jax.ShapeDtypeS...  12.5 us
    unnamed x37, local copies, waits for them, and re-layouts  8.82 us
  transfers between devices with their start and end apart: 15, of which 9 were waited for; matrix products, arithmetic and copies ran while one was open for 3% of the time, Pallas kernels for 18%

profile of v2, /device:TPU:0, one launch (start us, length us, event | category | flops | bytes accessed | tf_op | source)
XLA Modules:
  0.0 334.4 jit_solution(10241534528683863266)
XLA Ops:
  7.2 1.1 convert_element_type.116
  8.4 0.1 reshape.97
  8.5 0.3 fusion.3
  8.8 0.1 copy.29
  8.9 0.2 reshape_reshape.6
  9.2 0.1 reshape.98
  9.3 0.3 fusion.4
  9.6 0.1 copy.30
  9.8 0.2 reshape_reshape.7
  10.0 0.3 copy-done.10
  10.3 0.1 convert_element_type.122
  10.4 0.1 pad_maximum_fusion
  10.6 32.1 %all_to_all.10 = bf16[4,64,2048]{2,1,0:T(8,128)(2,1)} all-to-all(bf16[4,64,2048]{2,1,0:T(8,128)(2,1)S(1)} %pad_maximum_fusion), channel_id=1, replica_groups=mesh['dp'=8,'mp'=4] {'mp'}, dimensions={0} | all-to-all | bytes 2097152 | tf_op jit(solution)/shard_map/all_to_all | solution.py:245
  42.7 0.1 convert_element_type.123
  42.8 0.1 convert_element_type.124
  42.9 0.1 bitcast_bitcast_fusion.2
  43.0 0.1 pad_maximum_fusion.1
  43.1 28.2 %all_to_all.11 = bf16[4,64,2048]{2,1,0:T(8,128)(2,1)} all-to-all(bf16[4,64,2048]{2,1,0:T(8,128)(2,1)S(1)} %pad_maximum_fusion.1), channel_id=1, replica_groups=mesh['dp'=8,'mp'=4] {'mp'}, dimensions={0} | all-to-all | bytes 2097152 | tf_op jit(solution)/shard_map/all_to_all | solution.py:245
  71.3 0.3 collective-permute-start
  71.6 25.4 %collective-permute-done.refs_1_ = bf16[256,2048]{1,0:T(8,128)(2,1)} collective-permute-done((bf16[256,2048]{1,0:T(8,128)(2,1)S(1)}, bf16[256,2048]{1,0:T(8,128)(2,1)}, u32[]{:S(2)}, u32[]{:S(2)}) %collective-permute-start) | collective-permute-done | bytes 1048608 | tf_op jit(solution)/shard_map/ppermute | solution.py:274
  97.0 1.9 multiply_sine_fusion
  98.9 7.0 %project.4 = (bf16[1024,2048]{1,0:T(8,128)(2,1)}, bf16[1024,2048]{1,0:T(8,128)(2,1)}) custom-call(s32[1]{0:T(128)} %bitcast.11.refs_0_.scalars, bf16[256,2048]{1,0:T(8,128)(2,1)S(1)} %copy-done.4, f32[1,2048]{1,0:T(1,128)S(1)} %bitcast.72, f32[1024,128]{1,0:T(8,128)S(1)} %get-tuple-element.73.refs_3_, f32[1024,128]{1,0:T(8,128)S(1)} %get-tuple-element.72.refs_4_, ...), custom_call_target="tpu_custom_call" | custom-call | flops 2147483648 | bytes 10485760 | tf_op jit(solution)/shard_map/project/pallas_call | solution.py:119
  106.0 15.8 %collective-permute-done.1.refs_1_ = bf16[256,2048]{1,0:T(8,128)(2,1)S(1)} collective-permute-done((bf16[256,2048]{1,0:T(8,128)(2,1)}, bf16[256,2048]{1,0:T(8,128)(2,1)S(1)}, u32[]{:S(2)}, u32[]{:S(2)}) %collective-permute-start.1) | collective-permute-done | bytes 1048608 | tf_op jit(solution)/shard_map/ppermute | solution.py:274
  121.8 0.6 reduce-window.6
  122.3 0.2 slice_reduce_fusion
  122.5 0.2 reduce-window.9
  122.7 0.1 add_bitcast_fusion
  122.8 1.0 copy.38.refs_2_
  124.5 0.1 pad_add_fusion.refs_0_
  124.6 8.8 %project.5 = (bf16[1024,2048]{1,0:T(8,128)(2,1)}, bf16[1024,2048]{1,0:T(8,128)(2,1)}) custom-call(s32[1]{0:T(128)} %bitcast.14.refs_0_.scalars, bf16[256,2048]{1,0:T(8,128)(2,1)} %collective-permute-done.refs_1_, f32[1,2048]{1,0:T(1,128)S(1)} %bitcast.73, f32[1024,128]{1,0:T(8,128)S(1)} %get-tuple-element.73.refs_3_, ...), custom_call_target="tpu_custom_call", output_to_operand_aliasing={{0}: (6, {}), {1}: (7, {})} | custom-call | flops 2147483648 | bytes 10485760 | tf_op jit(solution)/shard_map/project/pallas_call | solution.py:119
  133.4 12.1 %collective-permute-done.2.refs_1_ = bf16[256,2048]{1,0:T(8,128)(2,1)} collective-permute-done((bf16[256,2048]{1,0:T(8,128)(2,1)S(1)}, bf16[256,2048]{1,0:T(8,128)(2,1)}, u32[]{:S(2)}, u32[]{:S(2)}) %collective-permute-start.2) | collective-permute-done | bytes 1048608 | tf_op jit(solution)/shard_map/ppermute | solution.py:274
  145.5 7.1 %project.6 = (bf16[1024,2048]{1,0:T(8,128)(2,1)}, bf16[1024,2048]{1,0:T(8,128)(2,1)}) custom-call(s32[1]{0:T(128)} %bitcast.13.refs_0_.scalars, bf16[256,2048]{1,0:T(8,128)(2,1)S(1)} %collective-permute-done.1.refs_1_, f32[1,2048]{1,0:T(1,128)S(1)} %bitcast.74, ...), custom_call_target="tpu_custom_call", output_to_operand_aliasing={{0}: (6, {}), {1}: (7, {})} | custom-call | flops 2147483648 | bytes 10485760 | tf_op jit(solution)/shard_map/project/pallas_call | solution.py:119
  152.6 7.4 %project.7 = (bf16[1024,2048]{1,0:T(8,128)(2,1)}, bf16[1024,2048]{1,0:T(8,128)(2,1)}) custom-call(s32[1]{0:T(128)} %bitcast.refs_0_, bf16[256,2048]{1,0:T(8,128)(2,1)} %collective-permute-done.2.refs_1_, f32[1,2048]{1,0:T(1,128)S(1)} %bitcast.75, f32[1024,128]{1,0:T(8,128)S(1)} %get-tuple-element.73.refs_3_, ...), custom_call_target="tpu_custom_call", output_to_operand_aliasing={{0}: (6, {}), {1}: (7, {})} | custom-call | flops 2147483648 | bytes 10485760 | tf_op jit(solution)/shard_map/project/pallas_call | solution.py:119
  160.1 1.1 copy-done.14
  161.2 0.1 convert_element_type.127
  161.3 0.1 fusion.6
  161.4 0.1 collective-permute-start.3
  161.5 0.1 collective-permute-start.4
  161.6 3.7 %collective-permute-start.5 = (bf16[64,2048]{1,0:T(8,128)(2,1)S(1)}, bf16[64,2048]{1,0:T(8,128)(2,1)S(1)}, u32[]{:S(2)}, u32[]{:S(2)}) collective-permute-start(bf16[64,2048]{1,0:T(8,128)(2,1)S(1)} %get-tuple-element.66), channel_id=1, source_target_pairs={{0,3},{1,0},{2,1},{3,2},{4,7},{5,4},{6,5},{7,6},{8,11},{9,8},{10,9... | collective-permute-start | bytes 786440 | tf_op jit(solution)/shard_map/ppermute | solution.py:64
  165.3 19.4 %retention.1 = bf16[1024,2048]{1,0:T(8,128)(2,1)S(1)} custom-call(s32[2]{0:T(128)S(1)} %pad_add_fusion.refs_0_, bf16[1024,2048]{1,0:T(8,128)(2,1)} %get-tuple-element.51.refs_1_, f32[1024,2]{1,0:T(8,128)S(1)} %copy-done.6, f32[2,1024]{1,0:T(2,128)S(1)} %bitcast.77, bf16[1024,2048]{1,0:T(8,128)(2,1)} %get-tuple-element.52.refs_4_, ...), custom_call_target="tpu_custom_call" | custom-call | flops 12000000000 | bytes 20000000 | tf_op jit(solution)/shard_map/retention/pallas_call | solution.py:191
  184.7 2.0 copy-done.5
  186.7 0.1 broadcast_in_dim.2
  187.0 1.0 copy-done.9
  188.0 1.3 constant_dynamic-slice_fusion
  189.3 0.6 collective-permute-start.6
  189.9 21.6 %collective-permute-done.6 = bf16[256,2048]{1,0:T(8,128)(2,1)S(1)} collective-permute-done((bf16[256,2048]{1,0:T(8,128)(2,1)S(1)}, bf16[256,2048]{1,0:T(8,128)(2,1)S(1)}, u32[]{:S(2)}, u32[]{:S(2)}) %collective-permute-start.6) | collective-permute-done | bytes 1048608 | tf_op jit(solution)/shard_map/ppermute | solution.py:78
  211.5 1.6 add_convert_fusion.2
  213.1 0.1 collective-permute-start.7
  213.2 21.4 %collective-permute-done.7 = bf16[256,2048]{1,0:T(8,128)(2,1)} collective-permute-done((bf16[256,2048]{1,0:T(8,128)(2,1)S(1)}, bf16[256,2048]{1,0:T(8,128)(2,1)}, u32[]{:S(2)}, u32[]{:S(2)}) %collective-permute-start.7) | collective-permute-done | bytes 1048608 | tf_op jit(solution)/shard_map/ppermute | solution.py:78
  234.6 2.0 add_convert_fusion.1
  236.6 0.1 collective-permute-start.8
  236.7 20.2 %collective-permute-done.8 = bf16[256,2048]{1,0:T(8,128)(2,1)S(1)} collective-permute-done((bf16[256,2048]{1,0:T(8,128)(2,1)S(1)}, bf16[256,2048]{1,0:T(8,128)(2,1)S(1)}, u32[]{:S(2)}, u32[]{:S(2)}) %collective-permute-start.8) | collective-permute-done | bytes 1048608 | tf_op jit(solution)/shard_map/ppermute | solution.py:78
  256.9 1.9 fusion
  258.8 1.0 copy-done.8
  259.8 0.3 fusion.2.x_ref
  260.1 0.3 collective-permute-start.9
  260.5 3.4 %copy-done.2 = bf16[2048,2048]{1,0:T(8,128)(2,1)S(1)} copy-done((bf16[2048,2048]{1,0:T(8,128)(2,1)S(1)}, bf16[2048,2048]{1,0:T(8,128)(2,1)}, u32[]{:S(2)}) %copy-start.2) | copy-done | bytes 8388632
  263.8 3.1 ffn.4.refs_0_
  267.0 16.8 %collective-permute-done.9.x_ref = bf16[256,2048]{1,0:T(8,128)(2,1)S(1)} collective-permute-done((bf16[256,2048]{1,0:T(8,128)(2,1)S(1)}, bf16[256,2048]{1,0:T(8,128)(2,1)S(1)}, u32[]{:S(2)}, u32[]{:S(2)}) %collective-permute-start.9) | collective-permute-done | bytes 1048608 | tf_op jit(solution)/shard_map/ppermute | solution.py:296
  283.7 3.1 ffn.5.refs_0_
  286.9 20.2 %collective-permute-done.10.x_ref = bf16[256,2048]{1,0:T(8,128)(2,1)S(1)} collective-permute-done((bf16[256,2048]{1,0:T(8,128)(2,1)S(1)}, bf16[256,2048]{1,0:T(8,128)(2,1)S(1)}, u32[]{:S(2)}, u32[]{:S(2)}) %collective-permute-start.10) | collective-permute-done | bytes 1048608 | tf_op jit(solution)/shard_map/ppermute | solution.py:296
  307.1 3.1 ffn.6.refs_0_
  310.2 14.5 %collective-permute-done.11.x_ref = bf16[256,2048]{1,0:T(8,128)(2,1)S(1)} collective-permute-done((bf16[256,2048]{1,0:T(8,128)(2,1)S(1)}, bf16[256,2048]{1,0:T(8,128)(2,1)S(1)}, u32[]{:S(2)}, u32[]{:S(2)}) %collective-permute-start.11) | collective-permute-done | bytes 1048608 | tf_op jit(solution)/shard_map/ppermute | solution.py:296
  324.7 3.1 ffn.7
  (62 shorter events, 0.7 us)
Async XLA Ops:
  7.2 114.6 %copy-start = (f32[1024,8]{0,1:T(8,128)S(1)}, f32[1024,8]{0,1:T(8,128)}, u32[]{:S(2)}) copy-start(f32[1024,8]{0,1:T(8,128)} %param.16) | copy-start | bytes 98308
  7.2 2.0 copy-start.15
  7.2 91.7 %all-gather.4.cloned.1.call-start = ((), (), s32[]{:S(2)}) async-start(), calls=%async_computation.2 | async-start | bytes 9437184 | tf_op jit(solution)/shard_map/all_gather | solution.py:262
  9.1 1.2 copy-start.10
  10.5 32.2 %copy-start.11 = (f32[64,4096]{1,0:T(8,128)S(1)}, f32[64,4096]{1,0:T(8,128)}, u32[]{:S(2)}) copy-start(f32[64,4096]{1,0:T(8,128)} %param.20) | copy-start | bytes 3145732
  10.6 32.2 %copy-start.12 = (f32[4096,64]{0,1:T(8,128)S(1)}, f32[4096,64]{0,1:T(8,128)}, u32[]{:S(2)}) copy-start(f32[4096,64]{0,1:T(8,128)} %param.21) | copy-start | bytes 3145732
  42.7 122.6 %all-gather.6.cloned.1.call-start = ((), (), s32[]{:S(2)}) async-start(), calls=%async_computation.3 | async-start | bytes 9437184 | tf_op jit(solution)/shard_map/all_gather | solution.py:267
  43.0 28.3 %copy-start.4 = (bf16[256,2048]{1,0:T(8,128)(2,1)S(1)}, bf16[256,2048]{1,0:T(8,128)(2,1)}, u32[]{:S(2)}) copy-start(bf16[256,2048]{1,0:T(8,128)(2,1)} %refs_1_) | copy-start | bytes 3145732
  43.1 55.8 %copy-start.7 = (f32[2048]{0:T(1024)S(1)}, f32[2048]{0:T(1024)}, u32[]{:S(2)}) copy-start(f32[2048]{0:T(1024)} %param.13) | copy-start | bytes 24580
  71.2 189.2 %all-gather.8.cloned.1.call-start = ((), (), s32[]{:S(2)}) async-start(), calls=%async_computation.4 | async-start | bytes 9437184 | tf_op jit(solution)/shard_map/all_gather | solution.py:289
  71.3 25.6 %collective-permute-start = (bf16[256,2048]{1,0:T(8,128)(2,1)S(1)}, bf16[256,2048]{1,0:T(8,128)(2,1)}, u32[]{:S(2)}, u32[]{:S(2)}) collective-permute-start(bf16[256,2048]{1,0:T(8,128)(2,1)S(1)} %copy-done.4), channel_id=1, source_target_pairs={{0,1},{1,2},{2,3},{3,0},{4,5},{5,6},{6,7},{7,4},{8,9},{9,10},{10,1... | collective-permute-start | bytes 3145736 | tf_op jit(solution)/shard_map/ppermute | solution.py:274
  97.0 24.8 %collective-permute-start.1 = (bf16[256,2048]{1,0:T(8,128)(2,1)}, bf16[256,2048]{1,0:T(8,128)(2,1)S(1)}, u32[]{:S(2)}, u32[]{:S(2)}) collective-permute-start(bf16[256,2048]{1,0:T(8,128)(2,1)} %collective-permute-done.refs_1_), channel_id=1, source_target_pairs={{0,1},{1,2},{2,3},{3,0},{4,5},{5,6},{6,7},{7,4},{8,9},{9,10},{10,1... | collective-permute-start | bytes 3145736 | tf_op jit(solution)/shard_map/ppermute | solution.py:274
  121.7 23.7 %collective-permute-start.2 = (bf16[256,2048]{1,0:T(8,128)(2,1)S(1)}, bf16[256,2048]{1,0:T(8,128)(2,1)}, u32[]{:S(2)}, u32[]{:S(2)}) collective-permute-start(bf16[256,2048]{1,0:T(8,128)(2,1)S(1)} %collective-permute-done.1.refs_1_), channel_id=1, source_target_pairs={{0,1},{1,2},{2,3},{3,0},{4,5},{5,6},{6,7},{7,4},{8,9},{9,10},{10,1... | collective-permute-start | bytes 3145736 | tf_op jit(solution)/shard_map/ppermute | solution.py:274
  152.6 7.4 %copy-start.13 = (f32[64,4096]{1,0:T(8,128)S(1)}, f32[64,4096]{1,0:T(8,128)}, u32[]{:S(2)}) copy-start(f32[64,4096]{1,0:T(8,128)} %param.23) | copy-start | bytes 3145732
  160.0 1.2 copy-start.14
  161.2 4.1 %copy-start.6 = (f32[1024,2]{1,0:T(8,128)S(1)}, f32[1024,2]{1,0:T(8,128)}, u32[]{:S(2)}) copy-start(f32[1024,2]{1,0:T(8,128)} %copy.38.refs_2_) | copy-start | bytes 24580
  161.4 25.3 %collective-permute-start.3 = (bf16[64,2048]{1,0:T(8,128)(2,1)S(1)}, bf16[64,2048]{1,0:T(8,128)(2,1)S(1)}, u32[]{:S(2)}, u32[]{:S(2)}) collective-permute-start(bf16[64,2048]{1,0:T(8,128)(2,1)S(1)} %get-tuple-element.68), channel_id=1, source_target_pairs={{0,1},{1,2},{2,3},{3,0},{4,5},{5,6},{6,7},{7,4},{8,9},{9,10},{10,1... | collective-permute-start | bytes 786440 | tf_op jit(solution)/shard_map/ppermute | solution.py:64
  161.5 25.3 %collective-permute-start.4 = (bf16[64,2048]{1,0:T(8,128)(2,1)S(1)}, bf16[64,2048]{1,0:T(8,128)(2,1)S(1)}, u32[]{:S(2)}, u32[]{:S(2)}) collective-permute-start(bf16[64,2048]{1,0:T(8,128)(2,1)S(1)} %get-tuple-element.69), channel_id=1, source_target_pairs={{0,2},{1,3},{2,0},{3,1},{4,6},{5,7},{6,4},{7,5},{8,10},{9,11},{10,... | collective-permute-start | bytes 786440 | tf_op jit(solution)/shard_map/ppermute | solution.py:64
  161.6 25.1 %collective-permute-start.5 = (bf16[64,2048]{1,0:T(8,128)(2,1)S(1)}, bf16[64,2048]{1,0:T(8,128)(2,1)S(1)}, u32[]{:S(2)}, u32[]{:S(2)}) collective-permute-start(bf16[64,2048]{1,0:T(8,128)(2,1)S(1)} %get-tuple-element.66), channel_id=1, source_target_pairs={{0,3},{1,0},{2,1},{3,2},{4,7},{5,4},{6,5},{7,6},{8,11},{9,8},{10,9... | collective-permute-start | bytes 786440 | tf_op jit(solution)/shard_map/ppermute | solution.py:64
  184.7 2.0 copy-start.5
  187.0 1.0 copy-start.9
  189.3 22.2 %collective-permute-start.6 = (bf16[256,2048]{1,0:T(8,128)(2,1)S(1)}, bf16[256,2048]{1,0:T(8,128)(2,1)S(1)}, u32[]{:S(2)}, u32[]{:S(2)}) collective-permute-start(bf16[256,2048]{1,0:T(8,128)(2,1)S(1)} %constant_dynamic-slice_fusion), channel_id=1, source_target_pairs={{0,1},{1,2},{2,3},{3,0},{4,5},{5,6},{6,7},{7,4},{8,9},{9,10},{10,1... | collective-permute-start | bytes 3145736 | tf_op jit(solution)/shard_map/ppermute | solution.py:78
  213.1 21.4 %collective-permute-start.7 = (bf16[256,2048]{1,0:T(8,128)(2,1)S(1)}, bf16[256,2048]{1,0:T(8,128)(2,1)}, u32[]{:S(2)}, u32[]{:S(2)}) collective-permute-start(bf16[256,2048]{1,0:T(8,128)(2,1)S(1)} %add_convert_fusion.2), channel_id=1, source_target_pairs={{0,1},{1,2},{2,3},{3,0},{4,5},{5,6},{6,7},{7,4},{8,9},{9,10},{10,1... | collective-permute-start | bytes 3145736 | tf_op jit(solution)/shard_map/ppermute | solution.py:78
  236.6 20.3 %collective-permute-start.8 = (bf16[256,2048]{1,0:T(8,128)(2,1)S(1)}, bf16[256,2048]{1,0:T(8,128)(2,1)S(1)}, u32[]{:S(2)}, u32[]{:S(2)}) collective-permute-start(bf16[256,2048]{1,0:T(8,128)(2,1)S(1)} %add_convert_fusion.1), channel_id=1, source_target_pairs={{0,1},{1,2},{2,3},{3,0},{4,5},{5,6},{6,7},{7,4},{8,9},{9,10},{10,1... | collective-permute-start | bytes 3145736 | tf_op jit(solution)/shard_map/ppermute | solution.py:78
  236.7 23.1 %copy-start.16 = (f32[2048]{0:T(1024)S(1)}, f32[2048]{0:T(1024)}, u32[]{:S(2)}) copy-start(f32[2048]{0:T(1024)} %param.14) | copy-start | bytes 24580
  258.8 1.0 copy-start.8
  260.1 23.6 %collective-permute-start.9 = (bf16[256,2048]{1,0:T(8,128)(2,1)S(1)}, bf16[256,2048]{1,0:T(8,128)(2,1)S(1)}, u32[]{:S(2)}, u32[]{:S(2)}) collective-permute-start(bf16[256,2048]{1,0:T(8,128)(2,1)S(1)} %fusion.2.x_ref), channel_id=1, source_target_pairs={{0,1},{1,2},{2,3},{3,0},{4,5},{5,6},{6,7},{7,4},{8,9},{9,10},{10,1... | collective-permute-start | bytes 3145736 | tf_op jit(solution)/shard_map/ppermute | solution.py:296
  260.5 3.4 %copy-start.2 = (bf16[2048,2048]{1,0:T(8,128)(2,1)S(1)}, bf16[2048,2048]{1,0:T(8,128)(2,1)}, u32[]{:S(2)}) copy-start(bf16[2048,2048]{1,0:T(8,128)(2,1)} %all-gather.8.cloned.1.call-done.w_ref) | copy-start | bytes 25165828
  263.8 19.9 %copy-start.3 = (bf16[2048,2048]{1,0:T(8,128)(2,1)S(1)}, bf16[2048,2048]{1,0:T(8,128)(2,1)}, u32[]{:S(2)}) copy-start(bf16[2048,2048]{1,0:T(8,128)(2,1)} %all-gather.8.cloned.1.call-done.w_ref) | copy-start | bytes 25165828
  283.7 23.3 %collective-permute-start.10 = (bf16[256,2048]{1,0:T(8,128)(2,1)S(1)}, bf16[256,2048]{1,0:T(8,128)(2,1)S(1)}, u32[]{:S(2)}, u32[]{:S(2)}) collective-permute-start(bf16[256,2048]{1,0:T(8,128)(2,1)S(1)} %collective-permute-done.9.x_ref), channel_id=1, source_target_pairs={{0,1},{1,2},{2,3},{3,0},{4,5},{5,6},{6,7},{7,4},{8,9},{9,10},{10,1... | collective-permute-start | bytes 3145736 | tf_op jit(solution)/shard_map/ppermute | solution.py:296
  307.1 17.6 %collective-permute-start.11 = (bf16[256,2048]{1,0:T(8,128)(2,1)S(1)}, bf16[256,2048]{1,0:T(8,128)(2,1)S(1)}, u32[]{:S(2)}, u32[]{:S(2)}) collective-permute-start(bf16[256,2048]{1,0:T(8,128)(2,1)S(1)} %collective-permute-done.10.x_ref), channel_id=1, source_target_pairs={{0,1},{1,2},{2,3},{3,0},{4,5},{5,6},{6,7},{7,4},{8,9},{9,10},{10,1... | collective-permute-start | bytes 3145736 | tf_op jit(solution)/shard_map/ppermute | solution.py:296
  324.7 3.1 copy-start.1
Sparse Core Ops, SparseCore 0:
  42.8 53.4 all-gather.3
  98.2 54.3 all-gather.5
  188.1 53.9 all-gather.7
